TPU v7x, 32 devices: a whole 2x2x4 slice. The times are simulated.
32 devices in a mesh: lon: 8 (over z, x), lat: 4 (over y, core).
Axes of the slice: x: 2, y: 2, z: 4, core: 2. Of those that a mesh axis runs over, the one named last changes fastest.
Arguments:
- model_variables: float32 [3, 64, 32, 1024], P(None, None, 'lat', 'lon'), may hold values from -6 to 6
- obs_cell: int32 [2, 64], replicated, may hold values from 0 to 32767
- obs_value: float32 [2, 64], replicated, may hold values from -8 to 8
- obs_variance: float32 [2, 64], replicated, may hold values from 0.2 to 2
- tile_mask: int32 [2, 64, 32], P(None, None, ('lon', 'lat')), may hold values 0 or 1
Outputs:
- analysis: float32 [3, 64, 32, 1024], P(None, None, 'lat', 'lon')
All inputs are finite; a program needn't handle non-finite values. No bound on the sum of `tile_mask` on one device may be relied on, other than what follows from the above.
Results may differ from a plain program's by a relative error of at most 0.00015.
Values sent between devices are 32-bit elements; how exact they have to be, the bound alone decides.
No kernel may reach another device: no remote copies, remote signals or barrier semaphores. Data moves between devices by JAX's collectives and lax.ppermute only.
A program may use at most 64 MiB of HBM per device.

v0:
```python
import jax
import jax.numpy as jnp
from jax import lax
from jax.sharding import PartitionSpec as P

STEPS = 4
NBATCH = 2
LOC_RADIUS = 256


CORIOLIS = 0.1
COURANT = 0.5
SMALL_EPSILON = 1e-06


def with_halo(cells, sides, width):
    for axis, dim in sides:
        count = lax.axis_size(axis)
        head = lax.slice_in_dim(cells, 0, width, axis=dim)
        tail = lax.slice_in_dim(cells, cells.shape[dim] - width, cells.shape[dim], axis=dim)
        cells = jnp.concatenate(
            [
                lax.ppermute(tail, axis, [(i, (i + 1) % count) for i in range(count)]),
                cells,
                lax.ppermute(head, axis, [((i + 1) % count, i) for i in range(count)]),
            ],
            axis=dim,
        )
    return cells


def increments(prior, value, variance, ensemble_snapshots):
    center = jnp.mean(prior)
    spread_dev = prior - center
    spread = jnp.sum(spread_dev * spread_dev) / (ensemble_snapshots - 1) + SMALL_EPSILON
    post = 1.0 / (1.0 / spread + 1.0 / variance)
    post_mean = post * (center / spread + value / variance)
    delta = post_mean - center + (jnp.sqrt(post / spread) - 1.0) * spread_dev
    slope = spread_dev / ((ensemble_snapshots - 1) * spread)
    return (delta, slope)


def inside_rows(count, first, total_rows):
    global_rows = first + jnp.arange(count, dtype=jnp.int32)
    return ((global_rows >= 0) & (global_rows < total_rows))[:, None]


def coriolis_rows(count, first, total_rows):
    rows = (first + jnp.arange(count, dtype=jnp.int32)).astype(jnp.float32)
    return (CORIOLIS * ((2.0 * rows + 1.0) / total_rows - 1.0))[:, None]


def body(model_variables, obs_cell, obs_value, obs_variance, tile_mask):
    ensemble_snapshots = model_variables.shape[1]
    rows_dev = model_variables.shape[2]
    cols_dev = model_variables.shape[3]
    latitude_index = lax.axis_index("lat")
    lon_index = lax.axis_index("lon")
    total_rows = rows_dev * lax.axis_size("lat")
    total_cols = cols_dev * lax.axis_size("lon")
    row_first = latitude_index * rows_dev
    col_first = lon_index * cols_dev
    inside = inside_rows(rows_dev + 2, row_first - 1, total_rows)
    coriolis = coriolis_rows(rows_dev, row_first, total_rows)
    surface_elevation, east, north = (model_variables[0], model_variables[1], model_variables[2])
    for step in range(STEPS):
        flows = with_halo(jnp.stack([east, north]), (("lon", 3), ("lat", 2)), 1)
        flows = jnp.where(inside, flows, 0.0)
        east_grad = 0.5 * (flows[0, :, 1:-1, 2:] - flows[0, :, 1:-1, :-2])
        meridional_slope = 0.5 * (flows[1, :, 2:, 1:-1] - flows[1, :, :-2, 1:-1])
        surface_elevation = surface_elevation - COURANT * (east_grad + meridional_slope)
        widened = with_halo(surface_elevation, (("lon", 2), ("lat", 1)), 1)
        widened = jnp.where(inside, widened, 0.0)
        east_next = (
            east
            + coriolis * north
            - COURANT * (0.5 * (widened[:, 1:-1, 2:] - widened[:, 1:-1, :-2]))
        )
        north = (
            north
            - coriolis * east
            - COURANT * (0.5 * (widened[:, 2:, 1:-1] - widened[:, :-2, 1:-1]))
        )
        east = east_next
    layered_arrays = jnp.stack([surface_elevation, east, north])
    centre_lat = row_first + rows_dev // 2
    central_longitude = col_first + cols_dev // 2
    for batch in range(NBATCH):
        cells = obs_cell[batch]
        obs_lat = cells // total_cols
        obs_lon = cells % total_cols
        lat_gap = obs_lat - centre_lat
        lon_gap = jnp.abs(obs_lon - central_longitude)
        lon_gap = jnp.minimum(lon_gap, total_cols - lon_gap)
        distance = (lat_gap * lat_gap + lon_gap * lon_gap).astype(jnp.float32)
        weights = tile_mask[batch][:, 0].astype(jnp.float32) / (
            1.0 + distance / (LOC_RADIUS * LOC_RADIUS)
        )
        local_lat = cells // total_cols - row_first
        local_lon = cells % total_cols - col_first
        owned = (
            (local_lat >= 0) & (local_lat < rows_dev) & (local_lon >= 0) & (local_lon < cols_dev)
        )
        picked = layered_arrays[0][
            :, jnp.clip(local_lat, 0, rows_dev - 1), jnp.clip(local_lon, 0, cols_dev - 1)
        ]
        owned, share = (owned, jnp.where(owned[:, None], jnp.transpose(picked), 0.0))
        link_share = jnp.where(owned[:, None], weights[None, :], 0.0)
        priors, links = lax.psum((share, link_share), ("lon", "lat"))
        current = priors
        values = obs_value[batch]
        variances = obs_variance[batch]

        def turn(k, carry):
            current, transform = carry
            delta, slope = increments(current[0 + k], values[k], variances[k], ensemble_snapshots)
            coef = links[:, k] * jnp.dot(current, slope, precision=lax.Precision.HIGHEST)
            current = current + coef[:, None] * delta[None, :]
            lifted = jnp.dot(transform, slope, precision=lax.Precision.HIGHEST)
            transform = transform + weights[k] * lifted[:, None] * delta[None, :]
            return (current, transform)

        start = (current, jnp.eye(ensemble_snapshots, dtype=jnp.float32))
        priors, transform = lax.fori_loop(0, values.shape[0], turn, start)
        flat = layered_arrays.reshape(3, ensemble_snapshots, rows_dev * cols_dev)
        flat = jnp.einsum("fmc,mn->fnc", flat, transform, precision=lax.Precision.HIGHEST)
        layered_arrays = flat.reshape(3, ensemble_snapshots, rows_dev, cols_dev)
    return layered_arrays


def solution(mesh):
    in_specs = (P(None, None, "lat", "lon"), P(), P(), P(), P(None, None, ("lon", "lat")))
    out_specs = P(None, None, "lat", "lon")
    return jax.shard_map(body, mesh=mesh, in_specs=in_specs, out_specs=out_specs, check_vma=False)
```

profile of v0, /device:TPU:0, one launch (start us, length us, event | category | flops | bytes accessed | tf_op | source)
XLA Modules:
  0.0 1125.0 jit_solution(7391654058803117018)
XLA Ops:
  1.7 3.0 collective-permute-start
  4.9 3.1 collective-permute-start.1
  9.5 1.7 collective-permute-start.3
  11.2 2.7 collective-permute-done.2
  16.6 3.5 collective-permute-start.5
  26.2 4.9 collective-permute-start.9
  31.0 1.6 collective-permute-done.8
  34.4 2.7 collective-permute-done.10
  38.9 4.8 collective-permute-start.13
  47.0 2.0 collective-permute-done.14
  50.1 4.8 collective-permute-start.17
  58.4 2.7 collective-permute-done.18
  63.5 4.8 collective-permute-start.21
  71.7 2.0 collective-permute-done.22
  74.5 4.8 collective-permute-start.25
  80.9 1.7 collective-permute-start.26
  82.7 2.7 collective-permute-done.26
  86.6 2.1 subtract_subtract_fusion
  89.7 4.8 collective-permute-start.29
  94.6 39.2 %all-reduce.1 = (f32[64,64]{1,0:T(8,128)S(1)}, f32[64,64]{1,0:T(8,128)S(1)}) all-reduce(f32[64,64]{1,0:T(8,128)S(1)} %get-tuple-element.482, f32[64,64]{1,0:T(8,128)S(1)} %get-tuple-element.481), channel_id=1, replica_groups=mesh['lon'=8,'lat'=4] {'lon','lat'}, use_global_device_ids=true, to_apply=%region_0.1 | all-reduce | flops 8192 | bytes 65536 | tf_op jit(solution)/shard_map/psum | solution.py:109
  134.0 1.7 collective-permute-start.31
  135.7 458.9 %while.34 = (s32[]{:T(128)}, f32[64,64]{1,0:T(8,128)S(1)}, f32[64,64]{1,0:T(8,128)S(1)}, f32[64,64]{0,1:T(8,128)S(1)}, f32[64]{0:T(128)S(1)}, /*index=5*/f32[64]...) while((s32[]{:T(128)}, f32[64,64]{1,0:T(8,128)S(1)}, ...), condition=%wide.region_5.6_spmd, body=%wide.region_2.5_spmd.sunk | while | flops 115344 | bytes 102053 | solution.py:124
  597.7 42.4 %all-reduce = (f32[64,64]{1,0:T(8,128)S(1)}, f32[64,64]{1,0:T(8,128)S(1)}) all-reduce(f32[64,64]{1,0:T(8,128)S(1)} %get-tuple-element.480, f32[64,64]{1,0:T(8,128)S(1)} %get-tuple-element.479), channel_id=1, replica_groups=mesh['lon'=8,'lat'=4] {'lon','lat'}, use_global_device_ids=true, to_apply=%region_6.7 | all-reduce | flops 8192 | bytes 65536 | tf_op jit(solution)/shard_map/psum | solution.py:109
  640.1 483.0 %while.35 = (s32[]{:T(128)}, f32[64,64]{1,0:T(8,128)S(1)}, f32[64,64]{1,0:T(8,128)S(1)}, f32[64,64]{0,1:T(8,128)S(1)}, f32[64]{0:T(128)S(1)}, /*index=5*/f32[64]...) while((s32[]{:T(128)}, f32[64,64]{1,0:T(8,128)S(1)}, ...), condition=%wide.region_11.12_spmd, body=%wide.region_8.11_spmd.sunk | while | flops 115344 | bytes 102053 | solution.py:124
  (1278 shorter events, 550.7 us)
Async XLA Ops:
  1.7 7.6 collective-permute-start
  9.4 4.5 collective-permute-start.2
  9.5 5.2 collective-permute-start.3
  15.1 6.6 collective-permute-start.4
  16.6 5.1 collective-permute-start.5
  26.1 6.5 collective-permute-start.8
  26.2 6.4 collective-permute-start.9
  32.6 4.5 collective-permute-start.10
  33.7 4.7 collective-permute-start.11
  38.8 6.4 collective-permute-start.12
  38.9 6.4 collective-permute-start.13
  50.1 6.5 collective-permute-start.16
  50.1 6.4 collective-permute-start.17
  56.6 4.5 collective-permute-start.18
  57.7 4.6 collective-permute-start.19
  63.4 6.4 collective-permute-start.20
  63.5 6.4 collective-permute-start.21
  74.4 6.5 collective-permute-start.24
  74.5 6.4 collective-permute-start.25
  80.9 4.5 collective-permute-start.26
  89.7 44.2 %collective-permute-start.28 = (f32[64,8,1]{0,2,1:T(1,128)S(1)}, f32[64,8,1]{0,2,1:T(1,128)S(1)}, u32[]{:S(2)}, u32[]{:S(2)}) collective-permute-start(f32[64,8,1]{0,2,1:T(1,128)S(1)} %get-tuple-element.460), channel_id=1, source_target_pairs={{0,4},{4,8},{8,12},{12,16},{16,20},{20,24},{24,28},{28,0},{1,5},{5... | collective-permute-start | bytes 6152 | tf_op jit(solution)/shard_map/ppermute | solution.py:23
  89.7 44.2 %collective-permute-start.29 = (f32[64,8,1]{0,2,1:T(1,128)S(1)}, f32[64,8,1]{0,2,1:T(1,128)S(1)}, u32[]{:S(2)}, u32[]{:S(2)}) collective-permute-start(f32[64,8,1]{0,2,1:T(1,128)S(1)} %get-tuple-element.461), channel_id=1, source_target_pairs={{4,0},{8,4},{12,8},{16,12},{20,16},{24,20},{28,24},{0,28},{5,1},{9... | collective-permute-start | bytes 6152 | tf_op jit(solution)/shard_map/ppermute | solution.py:25
  133.9 460.9 %collective-permute-start.30 = (f32[64,1,130]{0,2,1:T(8,128)S(1)}, f32[64,1,130]{0,2,1:T(8,128)S(1)}, u32[]{:S(2)}, u32[]{:S(2)}) collective-permute-start(f32[64,1,130]{0,2,1:T(8,128)S(1)} %get-tuple-element.452), channel_id=1, source_target_pairs={{0,1},{1,2},{2,3},{3,0},{4,5},{5,6},{6,7},{7,4},{8,9},{9,10},{10,1... | collective-permute-start | bytes 99848 | tf_op jit(solution)/shard_map/ppermute | solution.py:23
  134.0 460.8 %collective-permute-start.31 = (f32[64,1,130]{0,2,1:T(8,128)S(1)}, f32[64,1,130]{0,2,1:T(8,128)S(1)}, u32[]{:S(2)}, u32[]{:S(2)}) collective-permute-start(f32[64,1,130]{0,2,1:T(8,128)S(1)} %get-tuple-element.453), channel_id=1, source_target_pairs={{1,0},{2,1},{3,2},{0,3},{5,4},{6,5},{7,6},{4,7},{9,8},{10,9},{11,1... | collective-permute-start | bytes 99848 | tf_op jit(solution)/shard_map/ppermute | solution.py:25
  (18 other events, 670.4 us)
where the time goes:
time: 1140 us; the launch traced here: 1120 us
  loops' own time  430 us (38%)
  local copies, waits for them, and re-layouts  236 us (21%)
  other arithmetic  175 us (15%)
  matrix products  116 us (10%)
  blocking collectives  81.5 us (7%)
  starting transfers between devices  54.9 us (5%)
  waiting for transfers between devices  31.3 us (3%)
    another operation x2, loops' own time, body(): priors, transform = lax.fori_loop(0, values.shape[0], turn, start)  430 us
    dot_general x128, matrix products, turn(): lifted = jnp.dot(transform, slope, precision=lax.Precision.HIGHEST)  95.4 us
    psum x2, blocking collectives, body(): priors, links = lax.psum((share, link_share), ('lon', 'lat'))  81.5 us
    dynamic_slice x128, local copies, waits for them, and re-layouts, turn(): values[k]  78.4 us
    dynamic_slice x128, local copies, waits for them, and re-layouts, turn(): transform = transform + weights[k] * lifted[:, None] * delta[None, :]  76.7 us
    reduce_sum x128, other arithmetic, increments(): jnp.sum(spread_dev * spread_dev) / (ensemble_snapshots - 1) + SMALL_EPSILON  76.5 us
    reduce_sum x128, other arithmetic, increments(): center = jnp.mean(prior)  76 us
    dynamic_slice x128, local copies, waits for them, and re-layouts, turn(): variances[k]  73.6 us
  transfers between devices with their start and end apart: 32, of which 21 were waited for; matrix products, arithmetic and copies ran while one was open for 23% of the time, Pallas kernels for 0%

commit v1 on v0

v1 whole, which is shorter than its diff:
```python
import functools
import math

import jax
import jax.numpy as jnp
from jax import lax
from jax.experimental import pallas as pl
from jax.experimental.pallas import tpu as pltpu
from jax.sharding import PartitionSpec as P

STEPS = 4
NBATCH = 2
LOC_RADIUS = 256

CORIOLIS = 0.1
COURANT = 0.5
SMALL_EPSILON = 1e-06

SUB = 8
LANES = 128
STRIP = 8
PANEL = 4
JOINED = 4
PICKS = 4
HIGHEST = lax.Precision.HIGHEST
VMEM_LIMIT = 48 * 1024 * 1024
FORECAST_LIMIT = 53 * 1024 * 1024 + 320 * 1024


def dot(a, b):
    return jnp.dot(a, b, precision=HIGHEST, preferred_element_type=jnp.float32)


def dot_rows(a, b):
    return lax.dot_general(
        a, b, (((0,), (0,)), ((), ())), precision=HIGHEST, preferred_element_type=jnp.float32
    )


def forecast_kernel(
    groups, members, n_lat, n_lon, cell_hbm, mask_hbm, own_hbm,
    core_out, mid_out, cross_out, core_strip, mid_strip, cross_strip, share_ref, cell_out,
    heights, slots, state, cell_ref, mask_ref, own_ref, parts, up_strip, down_strip, small_sems, own_sems, out_sems,
):
    lat = lax.axis_index("lat")
    lon = lax.axis_index("lon")
    odd = lax.rem(lat, 2)
    total_rows = n_lat * SUB
    total_cols = n_lon * LANES
    lane = lax.broadcasted_iota(jnp.int32, (SUB, LANES), 1)
    scales, turns = [], []
    for row in range(-SUB, 2 * SUB):
        place = lat * SUB + row
        inside = jnp.logical_and(place >= 0, place < total_rows)
        spin = CORIOLIS * ((2.0 * place.astype(jnp.float32) + 1.0) / total_rows - 1.0)
        scales.append(jnp.where(inside, 0.5 * COURANT, 0.0))
        turns.append(jnp.where(inside, spin, 0.0))
    batches, count = cell_ref.shape
    slice_size = batches * count * JOINED // groups
    share_rows = SUB * SUB * JOINED

    def own_copy(turn):
        rows = pl.ds(pl.multiple_of(turn * share_rows, share_rows), share_rows)
        return pltpu.make_async_copy(own_hbm.at[:, rows], own_ref.at[:, rows], own_sems.at[turn])

    def part_copies(turn, rows):
        return [
            pltpu.make_async_copy(parts.at[part, :, :, rows], out.at[:, :, rows], out_sems.at[turn, place])
            for place, (part, out) in enumerate(((2 - 2 * odd, core_out), (1, mid_out), (2 * odd, cross_out)))
        ]

    def group_rows(turn):
        return pl.ds(pl.multiple_of(turn * SUB * JOINED, SUB * JOINED), SUB * JOINED)

    small = [
        pltpu.make_async_copy(source, target, small_sems.at[place])
        for place, (source, target) in enumerate((
            (cell_hbm, cell_ref), (cell_hbm, cell_out), (mask_hbm, mask_ref)
        ))
    ]
    own_copy(0).start()
    for copy in small:
        copy.start()
    for turn in range(1, groups // JOINED):
        own_copy(turn).start()
    for copy in small:
        copy.wait()

    def minus(a, b):
        if b is None:
            return a
        return -b if a is None else a - b

    def plus(a, b):
        if a is None or b is None:
            return b if a is None else a
        return a + b

    def times(scale, a):
        return None if a is None else scale * a

    def along(x):
        if x is None:
            return None
        return pltpu.roll(x, 2 * LANES - 1, 1) - pltpu.roll(x, 1, 1)

    def member_groups(turn, found):
        own_copy(turn).wait()
        first = turn * JOINED
        live = [dict() for _ in range(3)]

        def get(field, row):
            return state[field, row + SUB] if row in live[field] else None

        def put(field, row, value):
            if value is not None:
                live[field][row] = True
                state[field, row + SUB] = value

        for field in range(3):
            for row in range(SUB):
                pieces = [
                    own_ref[field, pl.ds((first + group) * SUB * SUB + row, SUB, stride=SUB), :]
                    for group in range(JOINED)
                ]
                main = jnp.concatenate(pieces, axis=0)
                put(field, row, jnp.concatenate([main, jnp.zeros_like(main)], axis=1))
        for step in range(STEPS):
            for row in range(-SUB, 2 * SUB):
                slope = plus(along(get(1, row)), minus(get(2, row + 1), get(2, row - 1)))
                put(0, row, minus(get(0, row), times(scales[row + SUB], slope)))
            for row in range(-SUB, 2 * SUB):
                east, north = get(1, row), get(2, row)
                slope = minus(get(0, row + 1), get(0, row - 1))
                put(1, row, minus(plus(east, times(turns[row + SUB], north)), times(scales[row + SUB], along(get(0, row)))))
                put(2, row, minus(minus(north, times(turns[row + SUB], east)), times(scales[row + SUB], slope)))

        for row in range(-SUB, 2 * SUB):
            part = row // SUB + 1
            for field in range(3):
                value = get(field, row)
                if value is None:
                    value = jnp.zeros((SUB * JOINED, 2 * LANES), jnp.float32)
                place = group_rows(turn)
                parts[part, field, row % SUB, place, :] = value[:, :LANES]
                strips = (up_strip, mid_strip, down_strip)[part]
                strip = strips[field, row % SUB]
                for group in range(JOINED):
                    halo = value[SUB * group:SUB * (group + 1), LANES:]
                    turned = pltpu.roll(halo, 2 * STRIP * (first + group) + STRIP, 1)
                    strip = jnp.where(lane // (2 * STRIP) == first + group, turned, strip)
                strips[field, row % SUB] = strip
                if field == 0:
                    heights[row + SUB, 0, place, :] = value[:, :LANES]
                    heights[row + SUB, 1, place, :] = value[:, LANES:]
        for copy in part_copies(turn, group_rows(turn)):
            copy.start()
        for extra in range(slice_size):
            index = turn * slice_size + extra
            cell = cell_ref[lax.div(index, count), lax.rem(index, count)]
            row = lax.div(cell, total_cols)
            col = cell - row * total_cols - lon * LANES
            row = row - lat * SUB + SUB
            col = jnp.where(col < 0, col + total_cols, col)
            west = col >= total_cols - STRIP
            near = jnp.logical_and(row > 0, row < 3 * SUB - 1)
            near = jnp.logical_and(near, jnp.logical_or(col < LANES + STRIP, west))
            ring = jnp.where(west, col + (2 * LANES - total_cols), col)
            slots[found] = (row * (2 * LANES) + ring) * LANES + index
            found = found + near.astype(jnp.int32)
        return found

    found = lax.fori_loop(0, groups // JOINED, member_groups, 0)
    core_strip[...] = jnp.where(odd == 1, up_strip[...], down_strip[...])
    cross_strip[...] = jnp.where(odd == 1, down_strip[...], up_strip[...])
    tiles = share_ref.shape[0] - members
    mine = lax.broadcasted_iota(jnp.int32, (tiles, LANES), 0) == lax.rem(lon * n_lat + lat, tiles)
    mask = jnp.concatenate([mask_ref[batch] for batch in range(batches)], axis=1).astype(jnp.float32)
    share_ref[members:, :] = jnp.where(mine, mask, 0.0)
    wide = lax.broadcasted_iota(jnp.int32, (members, LANES), 1)

    def pick(turn, share):
        for extra in range(PICKS):
            item = turn * PICKS + extra
            packed = jnp.where(item < found, slots[item], 0)
            index = packed & (LANES - 1)
            col = (packed >> 7) & (LANES - 1)
            slab = heights[packed >> 15, (packed >> 14) & 1]
            turned = pltpu.roll(slab, (index - col) & (LANES - 1), 1)
            share = jnp.where(wide == jnp.where(item < found, index, LANES), turned, share)
        return share

    share_ref[:members, :] = lax.fori_loop(
        0, lax.div(found + PICKS - 1, PICKS), pick, jnp.zeros((members, LANES), jnp.float32)
    )
    for turn in range(groups // JOINED):
        for copy in part_copies(turn, group_rows(turn)):
            copy.wait()


def batch_steps(
    values, variances, batch, count, own, other, lam_own, lam_other, lam_cols, offset, mean, spin,
    hist_other, hist_rows,
):
    groups = count // SUB
    own = [own[SUB * i:SUB * (i + 1)] for i in range(groups)]
    other = [other[SUB * i:SUB * (i + 1)] for i in range(groups)]

    def spread(x, row):
        return jnp.broadcast_to(x[row:row + 1], (SUB, LANES))

    def column(x, lane):
        return jnp.broadcast_to(x[:, lane:lane + 1], (SUB, LANES))

    for first in range(0, count, PANEL):
        home, base = divmod(first, SUB)
        live = range(home, groups)
        inside = range(PANEL)
        cols = [{i: column(own[i], first + q) for i in live} for q in inside]
        lams = [
            {i: column(lam_cols[SUB * i:SUB * (i + 1)], offset + first + q) for i in live} for q in inside
        ]
        block = {(a, b): spread(cols[b][home], base + a) for a in inside for b in inside if a <= b}
        means = [column(mean, first + q) for q in inside]
        for t in inside:
            k = first + t
            variance = jnp.full((SUB, LANES), variances[batch, k], jnp.float32)
            noise = variance * lax.rsqrt(variance)
            square = block[t, t]
            root = lax.rsqrt(square + (variance + SMALL_EPSILON))
            inverse = root * root
            below = 1.0 + noise * root
            guess = pl.reciprocal(below, approx=True)
            shrink = -inverse * (guess * (2.0 - below * guess))
            shift = (values[batch, k] - means[t]) * inverse
            row_own = spread(own[home], base + t)
            row_other = spread(other[home], base + t)
            seen_own = spread(lam_own[SUB * home:SUB * (home + 1)], base + t) * row_own
            seen_other = spread(lam_other[SUB * home:SUB * (home + 1)], base + t) * row_other
            hist_other[k:k + 1, :] = seen_other[:1]
            hist_rows[k:k + 1, :] = (shift * spin + shrink * row_own)[:1]
            mean = mean + shift * seen_own
            first_own = shrink * seen_own
            second_own = shrink * (row_own + square * first_own)
            first_other = shrink * seen_other
            second_other = shrink * (row_other + square * first_other)
            alpha, beta = {}, {}
            for q in range(t + 1, PANEL):
                linked = spread(lams[t][home], base + q) * block[t, q]
                alpha[q] = shrink * linked
                beta[q] = block[t, q] + square * alpha[q]
                means[q] = means[q] + shift * linked
            for a in range(t + 1, PANEL):
                for b in range(a, PANEL):
                    block[a, b] = (block[a, b] + alpha[b] * block[t, a]) + alpha[a] * beta[b]
            for i in live:
                g = cols[t][i]
                u = lams[t][i] * g
                scaled = shrink * u
                for q in range(t + 1, PANEL):
                    cols[q][i] = cols[q][i] + (g * alpha[q] + scaled * beta[q])
                own[i] = own[i] + (g * first_own + u * second_own)
                other[i] = other[i] + (g * first_other + u * second_other)


def filter_kernel(
    count, members, seen_ref, share_ref, geo_ref, geo_cols_ref, near_ref, chosen_ref, mine_ref,
    change_ref, hist_other, hist_rows, values, variances, sems,
):
    copies = [
        pltpu.make_async_copy(seen_ref.at[0], values, sems.at[0]),
        pltpu.make_async_copy(seen_ref.at[1], variances, sems.at[1]),
    ]
    for copy in copies:
        copy.start()
    picked = share_ref[:members, :]
    masks = share_ref[members:, :].astype(jnp.bfloat16)
    chosen = chosen_ref[...].astype(jnp.bfloat16)
    across = (((0,), (0,)), ((), ()))
    links = geo_ref[...] * lax.dot_general(masks, chosen, across, preferred_element_type=jnp.float32)
    lam_cols = geo_cols_ref[...] * lax.dot_general(chosen, masks, across, preferred_element_type=jnp.float32)
    mine = near_ref[...] * lax.dot_general(
        masks, mine_ref[...].astype(jnp.bfloat16), across, preferred_element_type=jnp.float32
    )
    left = lax.broadcasted_iota(jnp.int32, (count, LANES), 1) < count
    swapped = pltpu.roll(links, count, 1)
    eye = (
        lax.broadcasted_iota(jnp.int32, (members, members), 0)
        == lax.broadcasted_iota(jnp.int32, (members, members), 1)
    ).astype(jnp.float32)
    zeros = jnp.zeros((members, members), jnp.float32)

    spin = 1.0 / math.sqrt(members - 1.0)

    def begin(block):
        mean = jnp.sum(block, axis=0, keepdims=True) * (1.0 / members)
        return mean, (block - mean) * spin

    mean, apart = begin(picked)
    first, second = apart[:, :count], apart[:, count:]
    own = dot_rows(first, jnp.concatenate([first, eye], axis=1))
    other = dot_rows(first, jnp.concatenate([second * math.sqrt(members - 1.0), eye], axis=1))
    mean = jnp.broadcast_to(jnp.concatenate([mean[:, :count], mean[:, :count]], axis=1), (SUB, LANES))
    for copy in copies:
        copy.wait()
    batch_steps(
        values, variances, 0, count, own, other,
        jnp.where(left, links[:count], 0.0), jnp.where(left, swapped[:count], mine[:count]),
        lam_cols[:count], 0, mean, spin, hist_other, hist_rows,
    )
    moved = dot_rows(hist_rows[:, LANES - members:], hist_other[...])
    after = picked[:, count:] + moved[:, :count]
    change_one = moved[:, count:]

    mean, apart = begin(after)
    own = dot_rows(apart, jnp.concatenate([apart, eye], axis=1))
    other = jnp.concatenate([zeros, own[:, count:]], axis=1)
    mean = jnp.broadcast_to(jnp.concatenate([mean, mean], axis=1), (SUB, LANES))
    batch_steps(
        values, variances, 1, count, own, other,
        jnp.where(left, swapped[count:], 0.0), jnp.where(left, 0.0, mine[count:]),
        lam_cols[count:], count, mean, spin, hist_other, hist_rows,
    )
    change_two = dot_rows(hist_rows[:, LANES - members:], hist_other[:, LANES - members:])
    change_ref[...] = change_one + change_two + dot(change_two, change_one)


def apply_kernel(members, change_ref, mid_ref, core_ref, cross_ref, even_ref, odd_ref, out_hbm, out_ref, sems):
    change = change_ref[...]
    high = change.astype(jnp.bfloat16)
    low = (change - high.astype(jnp.float32)).astype(jnp.bfloat16)
    left = jnp.concatenate([high, high, low], axis=1)
    lane = lax.broadcasted_iota(jnp.int32, (SUB, LANES), 1)
    edge = jnp.logical_or(lane < STRIP, lane >= LANES - STRIP)
    even = (lane % (2 * STRIP) < STRIP) == (lax.rem(lax.axis_index("lon"), 2) == 0)

    def whole(field, row):
        main = mid_ref[field, row] + core_ref[field, row] + cross_ref[field, row]
        strip = jnp.where(even, even_ref[field, row], odd_ref[field, row])
        parts = []
        for group in range(members // SUB):
            turn = (2 * LANES - STRIP - 2 * STRIP * group) % LANES
            parts.append(jnp.where(edge, pltpu.roll(strip, turn, 1), 0.0))
        return main + jnp.concatenate(parts, axis=0)

    copies = [pltpu.make_async_copy(out_ref.at[field], out_hbm.at[field], sems.at[field]) for field in range(3)]
    for field in range(3):
        for row in range(0, SUB, 2):
            block = jnp.concatenate([whole(field, row), whole(field, row + 1)], axis=1)
            top = block.astype(jnp.bfloat16)
            rest = (block - top.astype(jnp.float32)).astype(jnp.bfloat16)
            right = jnp.concatenate([top, rest, top], axis=0)
            fresh = block + jnp.dot(left, right, preferred_element_type=jnp.float32)
            for extra in range(2):
                out_ref[field, pl.ds(row + extra, members, stride=SUB), :] = fresh[
                    :, extra * LANES:(extra + 1) * LANES
                ]
        copies[field].start()
    for copy in copies:
        copy.wait()


def closeness(lat_gap, lon_gap, total_cols):
    lon_gap = jnp.abs(lon_gap)
    lon_gap = jnp.minimum(lon_gap, total_cols - lon_gap)
    distance = (lat_gap * lat_gap + lon_gap * lon_gap).astype(jnp.float32)
    return 1.0 / (1.0 + distance / (LOC_RADIUS * LOC_RADIUS))


def body(model_variables, obs_cell, obs_value, obs_variance, tile_mask):
    members = model_variables.shape[1]
    rows_dev = model_variables.shape[2]
    cols_dev = model_variables.shape[3]
    count = obs_cell.shape[1]
    n_lat = lax.axis_size("lat")
    n_lon = lax.axis_size("lon")
    n_tiles = n_lat * n_lon
    lat = lax.axis_index("lat")
    lon = lax.axis_index("lon")
    total_cols = cols_dev * n_lon
    groups = members // SUB
    both = NBATCH * count
    vmem = pl.BlockSpec(memory_space=pltpu.VMEM)
    params = pltpu.CompilerParams(vmem_limit_bytes=VMEM_LIMIT)

    def array(*shape):
        return jax.ShapeDtypeStruct(shape, jnp.float32)

    wide = array(3, rows_dev, members, cols_dev)
    narrow = array(3, rows_dev, SUB, cols_dev)
    base = n_tiles // 4
    core_part, mid_part, cross_part, core_strip, mid_strip, cross_strip, share, seen_cell = pl.pallas_call(
        functools.partial(forecast_kernel, groups, members, n_lat, n_lon),
        out_shape=(wide,) * 3
        + (narrow,) * 3
        + (array(members + base, both), jax.ShapeDtypeStruct((NBATCH, count), jnp.int32)),
        in_specs=[pl.BlockSpec(memory_space=pl.ANY)] * 3,
        out_specs=(pl.BlockSpec(memory_space=pl.ANY),) * 3 + (vmem,) * 5,
        scratch_shapes=[
            pltpu.VMEM((3 * SUB, 2, members, LANES), jnp.float32),
            pltpu.SMEM((both + PICKS,), jnp.int32),
            pltpu.VMEM((3, 3 * SUB, SUB * JOINED, 2 * LANES), jnp.float32),
            pltpu.SMEM((NBATCH, count), jnp.int32),
            pltpu.VMEM((NBATCH, 1, count), jnp.int32),
            pltpu.VMEM((3, members * rows_dev, cols_dev), jnp.float32),
            pltpu.VMEM((3, 3, rows_dev, members, cols_dev), jnp.float32),
            pltpu.VMEM((3, rows_dev, SUB, cols_dev), jnp.float32),
            pltpu.VMEM((3, rows_dev, SUB, cols_dev), jnp.float32),
            pltpu.SemaphoreType.DMA((3,)),
            pltpu.SemaphoreType.DMA((groups // JOINED,)),
            pltpu.SemaphoreType.DMA((groups // JOINED, 3)),
        ],
        compiler_params=pltpu.CompilerParams(vmem_limit_bytes=FORECAST_LIMIT),
        name="forecast",
    )(
        obs_cell,
        jnp.swapaxes(tile_mask, 1, 2),
        model_variables.reshape(3, members * rows_dev, cols_dev),
    )

    def swap(x, axis, size, bit):
        return lax.ppermute(x, axis, [(i, i ^ (1 << bit)) for i in range(size)])

    def after(share, *others):
        return lax.optimization_barrier((share,) + others)

    core_pairs = [(i, i ^ 1) for i in range(n_lat)]
    cross_pairs = [p for i in range(1, n_lat - 1, 2) for p in ((i, i + 1), (i + 1, i))]
    even_pairs = [(i, i ^ 1) for i in range(n_lon)]
    odd_pairs = [p for i in range(1, n_lon, 2) for p in ((i, (i + 1) % n_lon), ((i + 1) % n_lon, i))]

    core_corner = lax.ppermute(core_strip, "lat", core_pairs)
    lat_bits = n_lat.bit_length() - 1
    lon_bits = n_lon.bit_length() - 1
    for bit in reversed(range(lat_bits)):
        share = share + swap(share, "lat", n_lat, bit)
        if bit == lat_bits - 1:
            share, cross_strip = after(share, cross_strip)
            cross_corner = lax.ppermute(cross_strip, "lat", cross_pairs)
    share, cross_part, obs_value, obs_variance = after(share, cross_part, obs_value, obs_variance)
    from_cross = lax.ppermute(cross_part, "lat", cross_pairs)
    seen = jnp.stack([obs_value, obs_variance])
    strips = mid_strip + core_corner + cross_corner
    for bit in range(lon_bits):
        if bit == lon_bits - 2:
            share, core_part = after(share, core_part)
            from_core = lax.ppermute(core_part, "lat", core_pairs)
        if bit == lon_bits - 1:
            share, strips = after(share, strips)
            from_even = lax.ppermute(strips, "lon", even_pairs)
            from_odd = lax.ppermute(strips, "lon", odd_pairs)
        other = swap(share, "lon", n_lon, bit)
        if bit < lon_bits - 2:
            share = share + other
        else:
            high = (lon >> bit) & 1
            mine, theirs = share[members:], other[members:]
            share = jnp.concatenate([
                share[:members] + other[:members],
                jnp.where(high == 1, theirs, mine),
                jnp.where(high == 1, mine, theirs),
            ])

    cells = seen_cell.reshape(both)
    obs_row = cells // total_cols
    obs_col = cells % total_cols
    home_lat = obs_row // rows_dev
    home_lon = obs_col // cols_dev
    centre_row = home_lat * rows_dev + rows_dev // 2
    centre_col = home_lon * cols_dev + cols_dev // 2
    geo = closeness(obs_row[:, None] - centre_row, obs_col[:, None] - centre_col, total_cols)
    geo_cols = closeness(obs_row - centre_row[:, None], obs_col - centre_col[:, None], total_cols)
    tiles = jnp.arange(n_tiles, dtype=jnp.int32)
    chosen = (tiles[:, None] == home_lon * n_lat + home_lat).astype(jnp.float32)
    near = closeness(
        obs_row - (lat * rows_dev + rows_dev // 2), obs_col - (lon * cols_dev + cols_dev // 2), total_cols
    )
    near = jnp.broadcast_to(near[:, None], (both, LANES))
    mine = jnp.broadcast_to((tiles == lon * n_lat + lat).astype(jnp.float32)[:, None], (n_tiles, LANES))

    change = pl.pallas_call(
        functools.partial(filter_kernel, count, members),
        out_shape=array(members, members),
        in_specs=[vmem] * 7,
        out_specs=vmem,
        scratch_shapes=[pltpu.VMEM((count, LANES), jnp.float32)] * 2
        + [pltpu.SMEM((NBATCH, count), jnp.float32)] * 2
        + [pltpu.SemaphoreType.DMA((2,))],
        compiler_params=params,
        name="filter",
    )(seen, share, geo, geo_cols, near, chosen, mine)

    out = pl.pallas_call(
        functools.partial(apply_kernel, members),
        out_shape=array(3, members * rows_dev, cols_dev),
        in_specs=[vmem] * 6,
        out_specs=pl.BlockSpec(memory_space=pl.ANY),
        scratch_shapes=[
            pltpu.VMEM((3, members * rows_dev, cols_dev), jnp.float32),
            pltpu.SemaphoreType.DMA((3,)),
        ],
        compiler_params=params,
        name="apply",
    )(change, mid_part, from_core, from_cross, from_even, from_odd)
    return out.reshape(3, members, rows_dev, cols_dev)


def solution(mesh):
    in_specs = (P(None, None, "lat", "lon"), P(), P(), P(), P(None, None, ("lon", "lat")))
    out_specs = P(None, None, "lat", "lon")
    return jax.shard_map(body, mesh=mesh, in_specs=in_specs, out_specs=out_specs, check_vma=False)
```

time: 1140 us -> 42.4 us (0.04); the launches traced: 1120 us -> 41.8 us
  loops' own time: 430 us -> 0 us
  local copies, waits for them, and re-layouts: 236 us -> 1.6 us
  other arithmetic: 175 us -> 0.27 us
  matrix products: 116 us -> 0 us
  blocking collectives: 81.5 us -> 0 us
  starting transfers between devices: 54.9 us -> 16.3 us
  waiting for transfers between devices: 31.3 us -> 3.41 us
  Pallas kernels: 0 us -> 20.1 us
    another operation x2 -> x0, loops' own time: 430 us -> none  [body(): priors, transform = lax.fori_loop(0, values.shape[0], turn, start)]
    dynamic_slice x384 -> x0, local copies, waits for them, and re-layouts: 229 us -> none  [the longest x128 78.4 us: turn(): values[k]]
    reduce_sum x256 -> x0, other arithmetic: 152 us -> none  [the longest x128 76.5 us: increments(): jnp.sum(spread_dev * spread_dev) / (ensemble_snapshots - 1) + SMALL_EPSILON]
    dot_general x258 -> x0, matrix products: 116 us -> none  [the longest x128 95.4 us: turn(): lifted = jnp.dot(transform, slope, precision=lax.Precision.HIGHEST)]
    psum x2 -> x0, blocking collectives: 81.5 us -> none  [body(): priors, links = lax.psum((share, link_share), ('lon', 'lat'))]
    ppermute x32 -> x11, starting transfers between devices: 54.9 us -> 16.3 us  [the longest x5 9.78 us: swap(): return lax.ppermute(x, axis, [(i, i ^ 1 << bit) for i in range(size)])]
    ppermute x32 -> x11, waiting for transfers between devices: 31.3 us -> 3.41 us  [the longest x5 3.4 us: swap(): return lax.ppermute(x, axis, [(i, i ^ 1 << bit) for i in range(size)])]
    pallas_call x0 -> x3, Pallas kernels: none -> 20.1 us  [the longest x1 10.8 us: body(): pl.pallas_call(functools.partial(filter_kernel, count, members), out_shap...]
  transfers between devices with their start and end apart: 32 -> 11, of which waited for: 21 -> 3; matrix products, arithmetic and copies ran while one was open for 23% -> 1% of each run, Pallas kernels for 0% -> 26%
where the time goes in v1:
time: 42.4 us; the launch traced here: 41.8 us
  Pallas kernels  20.1 us (47%)
  starting transfers between devices  16.3 us (38%)
  waiting for transfers between devices  3.41 us (8%)
  local copies, waits for them, and re-layouts  1.6 us (4%)
    pallas_call x1, Pallas kernels, body(): pl.pallas_call(functools.partial(filter_kernel, count, members), out_shap...  10.8 us
    ppermute x5, starting transfers between devices, swap(): return lax.ppermute(x, axis, [(i, i ^ 1 << bit) for i in range(size)])  9.78 us
    pallas_call x1, Pallas kernels, body(): pl.pallas_call(functools.partial(forecast_kernel, groups, members, n_lat,...  8.01 us
    ppermute x5, waiting for transfers between devices, swap(): return lax.ppermute(x, axis, [(i, i ^ 1 << bit) for i in range(size)])  3.4 us
    ppermute x1, starting transfers between devices, body(): from_core = lax.ppermute(core_part, 'lat', core_pairs)  2.31 us
    ppermute x1, starting transfers between devices, body(): from_even = lax.ppermute(strips, 'lon', even_pairs)  1.49 us
    unnamed x10, local copies, waits for them, and re-layouts  1.38 us
    ppermute x1, starting transfers between devices, body(): from_odd = lax.ppermute(strips, 'lon', odd_pairs)  1.32 us
  transfers between devices with their start and end apart: 11, of which 3 were waited for; matrix products, arithmetic and copies ran while one was open for 1% of the time, Pallas kernels for 26%

profile of v1, /device:TPU:0, one launch (start us, length us, event | category | flops | bytes accessed | tf_op | source)
XLA Modules:
  0.0 41.8 jit_solution(3545342416292441703)
XLA Ops:
  0.0 0.7 %copy-done.2 = s32[2,64,1]{1,2,0:T(1,128)S(1)} copy-done((s32[2,64,1]{1,2,0:T(1,128)S(1)}, s32[2,64,1]{1,2,0:T(1,128)}, u32[]{:S(2)}) %copy-start.2) | copy-done | bytes 536
  0.7 0.0 copy-done.1
  0.7 8.0 %forecast.1 = (f32[3,8,64,128]{3,2,1,0:T(8,128)}, f32[3,8,64,128]{3,2,1,0:T(8,128)}, f32[3,8,64,128]{3,2,1,0:T(8,128)}, f32[3,8,8,128]{3,2,1,0:T(8,128)S(1)}, f3...) custom-call(s32[2,64]{1,0:T(2,128)S(1)} %copy-done.1, ...), custom_call_target="tpu_custom_call" | custom-call | tf_op jit(solution)/shard_map/forecast/pallas_call | solution.py:392
  8.7 3.0 %collective-permute-start = (f32[72,128]{1,0:T(8,128)S(1)}, f32[72,128]{1,0:T(8,128)S(1)}, u32[]{:S(2)}, u32[]{:S(2)}) collective-permute-start(f32[72,128]{1,0:T(8,128)S(1)} %get-tuple-element.23), channel_id=1, source_target_pairs={{0,2},{1,3},{2,0},{3,1},{4,6},{5,7},{6,4},{7,5},{8,10},{9,11},{10,... | collective-permute-start | bytes 110600 | tf_op jit(solution)/shard_map/ppermute | solution.py:422
  11.8 0.1 reshape.257
  11.9 0.1 fusion.11
  12.1 1.6 %collective-permute-done = f32[72,128]{1,0:T(8,128)S(1)} collective-permute-done((f32[72,128]{1,0:T(8,128)S(1)}, f32[72,128]{1,0:T(8,128)S(1)}, u32[]{:S(2)}, u32[]{:S(2)}) %collective-permute-start) | collective-permute-done | bytes 36896 | tf_op jit(solution)/shard_map/ppermute | solution.py:422
  13.7 0.7 %collective-permute-start.5 = (f32[3,8,8,128]{3,2,1,0:T(8,128)S(1)}, f32[3,8,8,128]{3,2,1,0:T(8,128)S(1)}, u32[]{:S(2)}, u32[]{:S(2)}) collective-permute-start(f32[3,8,8,128]{3,2,1,0:T(8,128)S(1)} %get-tuple-element.34), channel_id=1, source_target_pairs={{1,2},{2,1},{5,6},{6,5},{9,10},{10,9},{13,14},{14,13},{17,18},{18,... | collective-permute-start | bytes 294920 | tf_op jit(solution)/shard_map/ppermute | solution.py:439
  14.4 0.5 %collective-permute-done.1 = f32[72,128]{1,0:T(8,128)S(1)} collective-permute-done((f32[72,128]{1,0:T(8,128)S(1)}, f32[72,128]{1,0:T(8,128)S(1)}, u32[]{:S(2)}, u32[]{:S(2)}) %collective-permute-start.1) | collective-permute-done | bytes 36896 | tf_op jit(solution)/shard_map/ppermute | solution.py:422
  14.9 2.0 %collective-permute-start.2 = (f32[72,128]{1,0:T(8,128)S(1)}, f32[72,128]{1,0:T(8,128)S(1)}, u32[]{:S(2)}, u32[]{:S(2)}) collective-permute-start(f32[72,128]{1,0:T(8,128)S(1)} %add.160), channel_id=1, source_target_pairs={{0,4},{4,0},{8,12},{12,8},{16,20},{20,16},{24,28},{28,24},{1,5},{5... | collective-permute-start | bytes 110600 | tf_op jit(solution)/shard_map/ppermute | solution.py:422
  16.9 0.7 %collective-permute-start.8 = (f32[3,8,64,128]{3,2,1,0:T(8,128)}, f32[3,8,64,128]{3,2,1,0:T(8,128)S(1)}, u32[]{:S(2)}, u32[]{:S(2)}) collective-permute-start(f32[3,8,64,128]{3,2,1,0:T(8,128)} %get-tuple-element.39), channel_id=1, source_target_pairs={{1,2},{2,1},{5,6},{6,5},{9,10},{10,9},{13,14},{14,13},{17,18},{18,... | collective-permute-start | bytes 2359304 | tf_op jit(solution)/shard_map/ppermute | solution.py:441
  17.6 1.3 %collective-permute-done.2 = f32[72,128]{1,0:T(8,128)S(1)} collective-permute-done((f32[72,128]{1,0:T(8,128)S(1)}, f32[72,128]{1,0:T(8,128)S(1)}, u32[]{:S(2)}, u32[]{:S(2)}) %collective-permute-start.2) | collective-permute-done | bytes 36896 | tf_op jit(solution)/shard_map/ppermute | solution.py:422
  18.9 2.1 %collective-permute-start.3 = (f32[72,128]{1,0:T(8,128)S(1)}, f32[72,128]{1,0:T(8,128)S(1)}, u32[]{:S(2)}, u32[]{:S(2)}) collective-permute-start(f32[72,128]{1,0:T(8,128)S(1)} %add.161), channel_id=1, source_target_pairs={{0,8},{4,12},{8,0},{12,4},{16,24},{20,28},{24,16},{28,20},{1,9},{5... | collective-permute-start | bytes 110600 | tf_op jit(solution)/shard_map/ppermute | solution.py:422
  21.0 2.3 %collective-permute-start.7 = (f32[3,8,64,128]{3,2,1,0:T(8,128)}, f32[3,8,64,128]{3,2,1,0:T(8,128)S(1)}, u32[]{:S(2)}, u32[]{:S(2)}) collective-permute-start(f32[3,8,64,128]{3,2,1,0:T(8,128)} %get-tuple-element.38), channel_id=1, source_target_pairs={{0,1},{1,0},{2,3},{3,2},{4,5},{5,4},{6,7},{7,6},{8,9},{9,8},{10,11... | collective-permute-start | bytes 2359304 | tf_op jit(solution)/shard_map/ppermute | solution.py:447
  23.3 0.0 collective-permute-done.4
  23.3 0.0 copy-start.4
  23.4 2.7 %collective-permute-start.6 = (f32[80,128]{1,0:T(8,128)S(1)}, f32[80,128]{1,0:T(8,128)S(1)}, u32[]{:S(2)}, u32[]{:S(2)}) collective-permute-start(f32[80,128]{1,0:T(8,128)S(1)} %pad_maximum_fusion.1), channel_id=1, source_target_pairs={{0,16},{4,20},{8,24},{12,28},{16,0},{20,4},{24,8},{28,12},{1,17},{... | collective-permute-start | bytes 122888 | tf_op jit(solution)/shard_map/ppermute | solution.py:422
  26.0 0.7 %copy-done.3 = f32[2,64]{1,0:T(2,128)S(1)} copy-done((f32[2,64]{1,0:T(2,128)S(1)}, f32[2,64]{1,0:T(2,128)}, u32[]{:S(2)}) %copy-start.3) | copy-done | bytes 536
  26.7 1.5 %collective-permute-start.9 = (f32[3,8,8,128]{3,2,1,0:T(8,128)S(1)}, f32[3,8,8,128]{3,2,1,0:T(8,128)S(1)}, u32[]{:S(2)}, u32[]{:S(2)}) collective-permute-start(f32[3,8,8,128]{3,2,1,0:T(8,128)S(1)} %add_add_fusion), channel_id=1, source_target_pairs={{0,4},{4,0},{8,12},{12,8},{16,20},{20,16},{24,28},{28,24},{1,5},{5... | collective-permute-start | bytes 294920 | tf_op jit(solution)/shard_map/ppermute | solution.py:450
  28.2 1.3 %collective-permute-start.10 = (f32[3,8,8,128]{3,2,1,0:T(8,128)S(1)}, f32[3,8,8,128]{3,2,1,0:T(8,128)S(1)}, u32[]{:S(2)}, u32[]{:S(2)}) collective-permute-start(f32[3,8,8,128]{3,2,1,0:T(8,128)S(1)} %add_add_fusion), channel_id=1, source_target_pairs={{4,8},{8,4},{12,16},{16,12},{20,24},{24,20},{28,0},{0,28},{5,9},{9... | collective-permute-start | bytes 294920 | tf_op jit(solution)/shard_map/ppermute | solution.py:451
  29.6 0.1 broadcast_in_dim.4.near_ref
  29.6 0.1 broadcast_in_dim.5.mine_ref
  29.7 10.8 %filter.1.change_ref = f32[64,64]{1,0:T(8,128)S(1)} custom-call(f32[2,2,64]{2,1,0:T(2,128)S(1)} %pad_maximum_fusion.2.seen_ref, f32[96,128]{1,0:T(8,128)S(1)} %pad_maximum_fusion.share_ref, f32[128,128]{1,0:T(8,128)S(1)} %get-tuple-element.51.geo_ref, f32[128,128]{1,0:T(8,128)S(1)} %get-tuple-element.50.geo_cols_ref, ...), custom_call_target="tpu_custom_call" | custom-call | tf_op jit(solution)/shard_map/filter/pallas_call | solution.py:481
  40.5 1.3 %apply.1 = f32[3,512,128]{2,1,0:T(8,128)} custom-call(f32[64,64]{1,0:T(8,128)S(1)} %filter.1.change_ref, f32[3,8,64,128]{3,2,1,0:T(8,128)S(1)} %copy-done, f32[3,8,64,128]{3,2,1,0:T(8,128)S(1)} %collective-permute-done.7.core_ref, f32[3,8,64,128]{3,2,1,0:T(8,128)S(1)} %collective-permute-done.8.cross_ref, ...), custom_call_target="tpu_custom_call" | custom-call | tf_op jit(solution)/shard_map/apply/pallas_call | solution.py:493
  (31 shorter events, 0.2 us)
Async XLA Ops:
  0.0 0.7 %copy-start.2 = (s32[2,64,1]{1,2,0:T(1,128)S(1)}, s32[2,64,1]{1,2,0:T(1,128)}, u32[]{:S(2)}) copy-start(s32[2,64,1]{1,2,0:T(1,128)} %param.9) | copy-start | bytes 1540
  0.0 0.7 %copy-start.1 = (s32[2,64]{1,0:T(2,128)S(1)}, s32[2,64]{1,0:T(2,128)}, u32[]{:S(2)}) copy-start(s32[2,64]{1,0:T(2,128)} %cell_hbm.1) | copy-start | bytes 1540
  8.7 5.0 %collective-permute-start = (f32[72,128]{1,0:T(8,128)S(1)}, f32[72,128]{1,0:T(8,128)S(1)}, u32[]{:S(2)}, u32[]{:S(2)}) collective-permute-start(f32[72,128]{1,0:T(8,128)S(1)} %get-tuple-element.23), channel_id=1, source_target_pairs={{0,2},{1,3},{2,0},{3,1},{4,6},{5,7},{6,4},{7,5},{8,10},{9,11},{10,... | collective-permute-start | bytes 110600 | tf_op jit(solution)/shard_map/ppermute | solution.py:422
  11.7 11.5 %collective-permute-start.4 = (f32[3,8,8,128]{3,2,1,0:T(8,128)S(1)}, f32[3,8,8,128]{3,2,1,0:T(8,128)S(1)}, u32[]{:S(2)}, u32[]{:S(2)}) collective-permute-start(f32[3,8,8,128]{3,2,1,0:T(8,128)S(1)} %get-tuple-element.33), channel_id=1, source_target_pairs={{0,1},{1,0},{2,3},{3,2},{4,5},{5,4},{6,7},{7,6},{8,9},{9,8},{10,11... | collective-permute-start | bytes 294920 | tf_op jit(solution)/shard_map/ppermute | solution.py:432
  12.0 28.5 %copy-start = (f32[3,8,64,128]{3,2,1,0:T(8,128)S(1)}, f32[3,8,64,128]{3,2,1,0:T(8,128)}, u32[]{:S(2)}) copy-start(f32[3,8,64,128]{3,2,1,0:T(8,128)} %get-tuple-element.37.mid_ref) | copy-start | bytes 2359300
  13.7 1.2 %collective-permute-start.1 = (f32[72,128]{1,0:T(8,128)S(1)}, f32[72,128]{1,0:T(8,128)S(1)}, u32[]{:S(2)}, u32[]{:S(2)}) collective-permute-start(f32[72,128]{1,0:T(8,128)S(1)} %add.159), channel_id=1, source_target_pairs={{0,1},{1,0},{2,3},{3,2},{4,5},{5,4},{6,7},{7,6},{8,9},{9,8},{10,11... | collective-permute-start | bytes 110600 | tf_op jit(solution)/shard_map/ppermute | solution.py:422
  13.7 9.5 %collective-permute-start.5 = (f32[3,8,8,128]{3,2,1,0:T(8,128)S(1)}, f32[3,8,8,128]{3,2,1,0:T(8,128)S(1)}, u32[]{:S(2)}, u32[]{:S(2)}) collective-permute-start(f32[3,8,8,128]{3,2,1,0:T(8,128)S(1)} %get-tuple-element.34), channel_id=1, source_target_pairs={{1,2},{2,1},{5,6},{6,5},{9,10},{10,9},{13,14},{14,13},{17,18},{18,... | collective-permute-start | bytes 294920 | tf_op jit(solution)/shard_map/ppermute | solution.py:439
  14.9 4.0 %collective-permute-start.2 = (f32[72,128]{1,0:T(8,128)S(1)}, f32[72,128]{1,0:T(8,128)S(1)}, u32[]{:S(2)}, u32[]{:S(2)}) collective-permute-start(f32[72,128]{1,0:T(8,128)S(1)} %add.160), channel_id=1, source_target_pairs={{0,4},{4,0},{8,12},{12,8},{16,20},{20,16},{24,28},{28,24},{1,5},{5... | collective-permute-start | bytes 110600 | tf_op jit(solution)/shard_map/ppermute | solution.py:422
  16.9 23.6 %collective-permute-start.8 = (f32[3,8,64,128]{3,2,1,0:T(8,128)}, f32[3,8,64,128]{3,2,1,0:T(8,128)S(1)}, u32[]{:S(2)}, u32[]{:S(2)}) collective-permute-start(f32[3,8,64,128]{3,2,1,0:T(8,128)} %get-tuple-element.39), channel_id=1, source_target_pairs={{1,2},{2,1},{5,6},{6,5},{9,10},{10,9},{13,14},{14,13},{17,18},{18,... | collective-permute-start | bytes 2359304 | tf_op jit(solution)/shard_map/ppermute | solution.py:441
  18.9 4.4 %collective-permute-start.3 = (f32[72,128]{1,0:T(8,128)S(1)}, f32[72,128]{1,0:T(8,128)S(1)}, u32[]{:S(2)}, u32[]{:S(2)}) collective-permute-start(f32[72,128]{1,0:T(8,128)S(1)} %add.161), channel_id=1, source_target_pairs={{0,8},{4,12},{8,0},{12,4},{16,24},{20,28},{24,16},{28,20},{1,9},{5... | collective-permute-start | bytes 110600 | tf_op jit(solution)/shard_map/ppermute | solution.py:422
  21.0 19.6 %collective-permute-start.7 = (f32[3,8,64,128]{3,2,1,0:T(8,128)}, f32[3,8,64,128]{3,2,1,0:T(8,128)S(1)}, u32[]{:S(2)}, u32[]{:S(2)}) collective-permute-start(f32[3,8,64,128]{3,2,1,0:T(8,128)} %get-tuple-element.38), channel_id=1, source_target_pairs={{0,1},{1,0},{2,3},{3,2},{4,5},{5,4},{6,7},{7,6},{8,9},{9,8},{10,11... | collective-permute-start | bytes 2359304 | tf_op jit(solution)/shard_map/ppermute | solution.py:447
  23.3 2.7 %copy-start.4 = (f32[2,64]{1,0:T(2,128)S(1)}, f32[2,64]{1,0:T(2,128)}, u32[]{:S(2)}) copy-start(f32[2,64]{1,0:T(2,128)} %param.7) | copy-start | bytes 1540
  23.4 6.2 %collective-permute-start.6 = (f32[80,128]{1,0:T(8,128)S(1)}, f32[80,128]{1,0:T(8,128)S(1)}, u32[]{:S(2)}, u32[]{:S(2)}) collective-permute-start(f32[80,128]{1,0:T(8,128)S(1)} %pad_maximum_fusion.1), channel_id=1, source_target_pairs={{0,16},{4,20},{8,24},{12,28},{16,0},{20,4},{24,8},{28,12},{1,17},{... | collective-permute-start | bytes 122888 | tf_op jit(solution)/shard_map/ppermute | solution.py:422
  26.0 0.7 %copy-start.3 = (f32[2,64]{1,0:T(2,128)S(1)}, f32[2,64]{1,0:T(2,128)}, u32[]{:S(2)}) copy-start(f32[2,64]{1,0:T(2,128)} %param.8) | copy-start | bytes 1540
  26.7 13.8 %collective-permute-start.9 = (f32[3,8,8,128]{3,2,1,0:T(8,128)S(1)}, f32[3,8,8,128]{3,2,1,0:T(8,128)S(1)}, u32[]{:S(2)}, u32[]{:S(2)}) collective-permute-start(f32[3,8,8,128]{3,2,1,0:T(8,128)S(1)} %add_add_fusion), channel_id=1, source_target_pairs={{0,4},{4,0},{8,12},{12,8},{16,20},{20,16},{24,28},{28,24},{1,5},{5... | collective-permute-start | bytes 294920 | tf_op jit(solution)/shard_map/ppermute | solution.py:450
  28.2 12.3 %collective-permute-start.10 = (f32[3,8,8,128]{3,2,1,0:T(8,128)S(1)}, f32[3,8,8,128]{3,2,1,0:T(8,128)S(1)}, u32[]{:S(2)}, u32[]{:S(2)}) collective-permute-start(f32[3,8,8,128]{3,2,1,0:T(8,128)S(1)} %add_add_fusion), channel_id=1, source_target_pairs={{4,8},{8,4},{12,16},{16,12},{20,24},{24,20},{28,0},{0,28},{5,9},{9... | collective-permute-start | bytes 294920 | tf_op jit(solution)/shard_map/ppermute | solution.py:451

commit v2 on v1

--- a/solution.py
+++ b/solution.py
@@ -19,8 +19,7 @@
 SUB = 8
 LANES = 128
 STRIP = 8
-PANEL = 4
-JOINED = 4
+PANEL = 8
 PICKS = 4
 HIGHEST = lax.Precision.HIGHEST
 VMEM_LIMIT = 48 * 1024 * 1024
@@ -40,7 +39,7 @@
 def forecast_kernel(
     groups, members, n_lat, n_lon, cell_hbm, mask_hbm, own_hbm,
     core_out, mid_out, cross_out, core_strip, mid_strip, cross_strip, share_ref, cell_out,
-    heights, slots, state, cell_ref, mask_ref, own_ref, parts, up_strip, down_strip, small_sems, own_sems, out_sems,
+    slots, state, cell_ref, mask_ref, own_ref, small_sems, own_sems, out_sems,
 ):
     lat = lax.axis_index("lat")
     lon = lax.axis_index("lon")
@@ -48,6 +47,9 @@
     total_rows = n_lat * SUB
     total_cols = n_lon * LANES
     lane = lax.broadcasted_iota(jnp.int32, (SUB, LANES), 1)
+    zone = ((lane + STRIP) & (LANES - 1)) // (2 * STRIP)
+    at_last = lane % (2 * STRIP) == 2 * STRIP - 1
+    at_first = lane % (2 * STRIP) == 0
     scales, turns = [], []
     for row in range(-SUB, 2 * SUB):
         place = lat * SUB + row
@@ -56,35 +58,17 @@
         scales.append(jnp.where(inside, 0.5 * COURANT, 0.0))
         turns.append(jnp.where(inside, spin, 0.0))
     batches, count = cell_ref.shape
-    slice_size = batches * count * JOINED // groups
-    share_rows = SUB * SUB * JOINED
-
-    def own_copy(turn):
-        rows = pl.ds(pl.multiple_of(turn * share_rows, share_rows), share_rows)
-        return pltpu.make_async_copy(own_hbm.at[:, rows], own_ref.at[:, rows], own_sems.at[turn])
-
-    def part_copies(turn, rows):
-        return [
-            pltpu.make_async_copy(parts.at[part, :, :, rows], out.at[:, :, rows], out_sems.at[turn, place])
-            for place, (part, out) in enumerate(((2 - 2 * odd, core_out), (1, mid_out), (2 * odd, cross_out)))
-        ]
-
-    def group_rows(turn):
-        return pl.ds(pl.multiple_of(turn * SUB * JOINED, SUB * JOINED), SUB * JOINED)
-
+    own_copies = [
+        pltpu.make_async_copy(own_hbm.at[field], own_ref.at[field], own_sems.at[field]) for field in (1, 2, 0)
+    ]
     small = [
         pltpu.make_async_copy(source, target, small_sems.at[place])
         for place, (source, target) in enumerate((
             (cell_hbm, cell_ref), (cell_hbm, cell_out), (mask_hbm, mask_ref)
         ))
     ]
-    own_copy(0).start()
-    for copy in small:
+    for copy in own_copies + small:
         copy.start()
-    for turn in range(1, groups // JOINED):
-        own_copy(turn).start()
-    for copy in small:
-        copy.wait()
 
     def minus(a, b):
         if b is None:
@@ -102,62 +86,33 @@
     def along(x):
         if x is None:
             return None
-        return pltpu.roll(x, 2 * LANES - 1, 1) - pltpu.roll(x, 1, 1)
-
-    def member_groups(turn, found):
-        own_copy(turn).wait()
-        first = turn * JOINED
-        live = [dict() for _ in range(3)]
-
-        def get(field, row):
-            return state[field, row + SUB] if row in live[field] else None
-
-        def put(field, row, value):
-            if value is not None:
-                live[field][row] = True
-                state[field, row + SUB] = value
-
-        for field in range(3):
-            for row in range(SUB):
-                pieces = [
-                    own_ref[field, pl.ds((first + group) * SUB * SUB + row, SUB, stride=SUB), :]
-                    for group in range(JOINED)
-                ]
-                main = jnp.concatenate(pieces, axis=0)
-                put(field, row, jnp.concatenate([main, jnp.zeros_like(main)], axis=1))
-        for step in range(STEPS):
-            for row in range(-SUB, 2 * SUB):
-                slope = plus(along(get(1, row)), minus(get(2, row + 1), get(2, row - 1)))
-                put(0, row, minus(get(0, row), times(scales[row + SUB], slope)))
-            for row in range(-SUB, 2 * SUB):
-                east, north = get(1, row), get(2, row)
-                slope = minus(get(0, row + 1), get(0, row - 1))
-                put(1, row, minus(plus(east, times(turns[row + SUB], north)), times(scales[row + SUB], along(get(0, row)))))
-                put(2, row, minus(minus(north, times(turns[row + SUB], east)), times(scales[row + SUB], slope)))
-
-        for row in range(-SUB, 2 * SUB):
-            part = row // SUB + 1
-            for field in range(3):
-                value = get(field, row)
-                if value is None:
-                    value = jnp.zeros((SUB * JOINED, 2 * LANES), jnp.float32)
-                place = group_rows(turn)
-                parts[part, field, row % SUB, place, :] = value[:, :LANES]
-                strips = (up_strip, mid_strip, down_strip)[part]
-                strip = strips[field, row % SUB]
-                for group in range(JOINED):
-                    halo = value[SUB * group:SUB * (group + 1), LANES:]
-                    turned = pltpu.roll(halo, 2 * STRIP * (first + group) + STRIP, 1)
-                    strip = jnp.where(lane // (2 * STRIP) == first + group, turned, strip)
-                strips[field, row % SUB] = strip
-                if field == 0:
-                    heights[row + SUB, 0, place, :] = value[:, :LANES]
-                    heights[row + SUB, 1, place, :] = value[:, LANES:]
-        for copy in part_copies(turn, group_rows(turn)):
-            copy.start()
-        for extra in range(slice_size):
-            index = turn * slice_size + extra
-            cell = cell_ref[lax.div(index, count), lax.rem(index, count)]
+        right, left = pltpu.roll(x, LANES - 1, 1), pltpu.roll(x, 1, 1)
+        rights = [right[SUB * g:SUB * (g + 1)] for g in range(groups + 1)]
+        lefts = [left[SUB * g:SUB * (g + 1)] for g in range(groups + 1)]
+        first, last = rights[0], lefts[0]
+        for g in range(1, groups):
+            first = jnp.where(zone == g, rights[g], first)
+            last = jnp.where(zone == g, lefts[g], last)
+        mend = jnp.where(at_last, rights[groups] - first, jnp.where(at_first, last - lefts[groups], 0.0))
+        parts = [rights[g] - lefts[g] + jnp.where(zone == g, mend, 0.0) for g in range(groups)]
+        parts.append(
+            jnp.where(at_last, first, rights[groups]) - jnp.where(at_first, last, lefts[groups])
+        )
+        return jnp.concatenate(parts, axis=0)
+
+    live = [dict() for _ in range(3)]
+
+    def get(field, row):
+        return state[field, row + SUB] if row in live[field] else None
+
+    def put(field, row, value):
+        if value is not None:
+            live[field][row] = True
+            state[field, row + SUB] = value
+
+    def list_cells(start, stop, found):
+        for index in range(start, stop):
+            cell = cell_ref[index // count, index % count]
             row = lax.div(cell, total_cols)
             col = cell - row * total_cols - lon * LANES
             row = row - lat * SUB + SUB
@@ -170,9 +125,54 @@
             found = found + near.astype(jnp.int32)
         return found
 
-    found = lax.fori_loop(0, groups // JOINED, member_groups, 0)
-    core_strip[...] = jnp.where(odd == 1, up_strip[...], down_strip[...])
-    cross_strip[...] = jnp.where(odd == 1, down_strip[...], up_strip[...])
+    for copy in small:
+        copy.wait()
+    for field, copy in zip((1, 2, 0), own_copies):
+        copy.wait()
+        for row in range(SUB):
+            pieces = [
+                own_ref[field, pl.ds(group * SUB * SUB + row, SUB, stride=SUB), :] for group in range(groups)
+            ]
+            pieces = [pieces[0]] + [pltpu.roll(pieces[g], 2 * STRIP * g, 1) for g in range(1, groups)]
+            put(field, row, jnp.concatenate(pieces + [jnp.zeros((SUB, LANES), jnp.float32)], axis=0))
+
+    cells = batches * count
+    part_rows = [2 * SUB - 2 * SUB * odd, SUB, 2 * SUB * odd]
+    outs = [core_out, mid_out, cross_out]
+
+    def out_copy(part, fields):
+        rows = pl.ds(part_rows[part], SUB)
+        return pltpu.make_async_copy(
+            state.at[fields, rows, pl.ds(0, members)], outs[part].at[fields],
+            out_sems.at[part, 0 if fields.size == 1 else 1],
+        )
+
+    for row in (-SUB, 2 * SUB - 1):
+        for field in range(2):
+            state[field, row + SUB] = jnp.zeros((members + SUB, LANES), jnp.float32)
+    found = jnp.int32(0)
+    for step in range(STEPS):
+        for row in range(-SUB, 2 * SUB):
+            slope = plus(along(get(1, row)), minus(get(2, row + 1), get(2, row - 1)))
+            put(0, row, minus(get(0, row), times(scales[row + SUB], slope)))
+        found = list_cells(cells * step // STEPS, cells * (step + 1) // STEPS, found)
+        if step == STEPS - 1:
+            for part in range(3):
+                out_copy(part, pl.ds(0, 1)).start()
+        for row in range(-SUB, 2 * SUB):
+            east, north = get(1, row), get(2, row)
+            slope = minus(get(0, row + 1), get(0, row - 1))
+            put(1, row, minus(plus(east, times(turns[row + SUB], north)), times(scales[row + SUB], along(get(0, row)))))
+            put(2, row, minus(minus(north, times(turns[row + SUB], east)), times(scales[row + SUB], slope)))
+    for part in range(3):
+        out_copy(part, pl.ds(1, 2)).start()
+
+    halo = pl.ds(members, SUB)
+    for field in range(3):
+        up, down = state[field, pl.ds(0, SUB), halo, :], state[field, pl.ds(2 * SUB, SUB), halo, :]
+        mid_strip[field] = state[field, pl.ds(SUB, SUB), halo, :]
+        core_strip[field] = jnp.where(odd == 1, up, down)
+        cross_strip[field] = jnp.where(odd == 1, down, up)
     tiles = share_ref.shape[0] - members
     mine = lax.broadcasted_iota(jnp.int32, (tiles, LANES), 0) == lax.rem(lon * n_lat + lat, tiles)
     mask = jnp.concatenate([mask_ref[batch] for batch in range(batches)], axis=1).astype(jnp.float32)
@@ -184,30 +184,38 @@
             item = turn * PICKS + extra
             packed = jnp.where(item < found, slots[item], 0)
             index = packed & (LANES - 1)
-            col = (packed >> 7) & (LANES - 1)
-            slab = heights[packed >> 15, (packed >> 14) & 1]
-            turned = pltpu.roll(slab, (index - col) & (LANES - 1), 1)
+            ring = (packed >> 7) & (2 * LANES - 1)
+            row = packed >> 15
+            pieces = []
+            for group in range(groups):
+                place = pl.multiple_of(jnp.where(ring < LANES, group * SUB, members), SUB)
+                piece = state[0, row, pl.ds(place, SUB), :]
+                pieces.append(pltpu.roll(piece, (index - ring - 2 * STRIP * group) & (LANES - 1), 1))
+            turned = jnp.concatenate(pieces, axis=0)
             share = jnp.where(wide == jnp.where(item < found, index, LANES), turned, share)
         return share
 
     share_ref[:members, :] = lax.fori_loop(
         0, lax.div(found + PICKS - 1, PICKS), pick, jnp.zeros((members, LANES), jnp.float32)
     )
-    for turn in range(groups // JOINED):
-        for copy in part_copies(turn, group_rows(turn)):
-            copy.wait()
+    for part in range(3):
+        out_copy(part, pl.ds(0, 1)).wait()
+        out_copy(part, pl.ds(1, 2)).wait()
 
 
 def batch_steps(
     values, variances, batch, count, own, other, lam_own, lam_other, lam_cols, offset, mean, spin,
-    hist_other, hist_rows,
+    hist_other, hist_rows, lam_rows, spare,
 ):
     groups = count // SUB
     own = [own[SUB * i:SUB * (i + 1)] for i in range(groups)]
     other = [other[SUB * i:SUB * (i + 1)] for i in range(groups)]
 
-    def spread(x, row):
-        return jnp.broadcast_to(x[row:row + 1], (SUB, LANES))
+    lam_rows[batch, 0] = lam_own
+    lam_rows[batch, 1] = lam_other
+
+    def lam_row(side, k):
+        return jnp.broadcast_to(lam_rows[batch, side, k:k + 1, :], (SUB, LANES))
 
     def column(x, lane):
         return jnp.broadcast_to(x[:, lane:lane + 1], (SUB, LANES))
@@ -220,23 +228,39 @@
         lams = [
             {i: column(lam_cols[SUB * i:SUB * (i + 1)], offset + first + q) for i in live} for q in inside
         ]
-        block = {(a, b): spread(cols[b][home], base + a) for a in inside for b in inside if a <= b}
+        place = batch * groups + home
+
+        def keep(slot, x):
+            spare[place, slot] = x
+
+        def spread(slot, row):
+            return jnp.broadcast_to(spare[place, slot, row:row + 1, :], (SUB, LANES))
+
+        for q in inside:
+            keep(q, cols[q][home])
+        keep(2 * PANEL, own[home])
+        keep(2 * PANEL + 1, other[home])
+        for q in inside:
+            keep(PANEL + q, lams[q][home])
+        block = {(a, b): spread(b, base + a) for a in inside for b in inside if a <= b}
+        rows_own = [spread(2 * PANEL, base + q) for q in inside]
+        rows_other = [spread(2 * PANEL + 1, base + q) for q in inside]
         means = [column(mean, first + q) for q in inside]
+        noises = [jnp.full((SUB, LANES), variances[batch, first + q], jnp.float32) for q in inside]
+        total = block[0, 0] + (noises[0] + SMALL_EPSILON)
         for t in inside:
             k = first + t
-            variance = jnp.full((SUB, LANES), variances[batch, k], jnp.float32)
-            noise = variance * lax.rsqrt(variance)
+            noise = noises[t] * lax.rsqrt(noises[t])
             square = block[t, t]
-            root = lax.rsqrt(square + (variance + SMALL_EPSILON))
+            root = lax.rsqrt(total)
             inverse = root * root
             below = 1.0 + noise * root
             guess = pl.reciprocal(below, approx=True)
-            shrink = -inverse * (guess * (2.0 - below * guess))
+            shrink = (inverse * guess) * (below * guess - 2.0)
             shift = (values[batch, k] - means[t]) * inverse
-            row_own = spread(own[home], base + t)
-            row_other = spread(other[home], base + t)
-            seen_own = spread(lam_own[SUB * home:SUB * (home + 1)], base + t) * row_own
-            seen_other = spread(lam_other[SUB * home:SUB * (home + 1)], base + t) * row_other
+            row_own, row_other = rows_own[t], rows_other[t]
+            seen_own = lam_row(0, k) * row_own
+            seen_other = lam_row(1, k) * row_other
             hist_other[k:k + 1, :] = seen_other[:1]
             hist_rows[k:k + 1, :] = (shift * spin + shrink * row_own)[:1]
             mean = mean + shift * seen_own
@@ -245,15 +269,21 @@
             first_other = shrink * seen_other
             second_other = shrink * (row_other + square * first_other)
             alpha, beta = {}, {}
+            if t + 1 < PANEL:
+                linked = spread(PANEL + t, base + t + 1) * block[t, t + 1]
+                flat = block[t + 1, t + 1] + (noises[t + 1] + SMALL_EPSILON)
+                total = flat + shrink * (2.0 * (linked * block[t, t + 1]) + shrink * (linked * linked * square))
             for q in range(t + 1, PANEL):
-                linked = spread(lams[t][home], base + q) * block[t, q]
+                linked = spread(PANEL + t, base + q) * block[t, q]
                 alpha[q] = shrink * linked
                 beta[q] = block[t, q] + square * alpha[q]
+                rows_own[q] = rows_own[q] + (block[t, q] * first_own + linked * second_own)
+                rows_other[q] = rows_other[q] + (block[t, q] * first_other + linked * second_other)
                 means[q] = means[q] + shift * linked
             for a in range(t + 1, PANEL):
                 for b in range(a, PANEL):
                     block[a, b] = (block[a, b] + alpha[b] * block[t, a]) + alpha[a] * beta[b]
-            for i in live:
+            for i in live[1:]:
                 g = cols[t][i]
                 u = lams[t][i] * g
                 scaled = shrink * u
@@ -265,7 +295,7 @@
 
 def filter_kernel(
     count, members, seen_ref, share_ref, geo_ref, geo_cols_ref, near_ref, chosen_ref, mine_ref,
-    change_ref, hist_other, hist_rows, values, variances, sems,
+    change_ref, hist_other, hist_rows, lam_rows, spare, values, variances, sems,
 ):
     copies = [
         pltpu.make_async_copy(seen_ref.at[0], values, sems.at[0]),
@@ -306,7 +336,7 @@
     batch_steps(
         values, variances, 0, count, own, other,
         jnp.where(left, links[:count], 0.0), jnp.where(left, swapped[:count], mine[:count]),
-        lam_cols[:count], 0, mean, spin, hist_other, hist_rows,
+        lam_cols[:count], 0, mean, spin, hist_other, hist_rows, lam_rows, spare,
     )
     moved = dot_rows(hist_rows[:, LANES - members:], hist_other[...])
     after = picked[:, count:] + moved[:, :count]
@@ -319,7 +349,7 @@
     batch_steps(
         values, variances, 1, count, own, other,
         jnp.where(left, swapped[count:], 0.0), jnp.where(left, 0.0, mine[count:]),
-        lam_cols[count:], count, mean, spin, hist_other, hist_rows,
+        lam_cols[count:], count, mean, spin, hist_other, hist_rows, lam_rows, spare,
     )
     change_two = dot_rows(hist_rows[:, LANES - members:], hist_other[:, LANES - members:])
     change_ref[...] = change_one + change_two + dot(change_two, change_one)
@@ -331,17 +361,17 @@
     low = (change - high.astype(jnp.float32)).astype(jnp.bfloat16)
     left = jnp.concatenate([high, high, low], axis=1)
     lane = lax.broadcasted_iota(jnp.int32, (SUB, LANES), 1)
-    edge = jnp.logical_or(lane < STRIP, lane >= LANES - STRIP)
-    even = (lane % (2 * STRIP) < STRIP) == (lax.rem(lax.axis_index("lon"), 2) == 0)
+    zone = ((lane + STRIP) & (LANES - 1)) // (2 * STRIP)
+    even = (lane % (2 * STRIP) >= STRIP) == (lax.rem(lax.axis_index("lon"), 2) == 0)
 
     def whole(field, row):
         main = mid_ref[field, row] + core_ref[field, row] + cross_ref[field, row]
         strip = jnp.where(even, even_ref[field, row], odd_ref[field, row])
         parts = []
         for group in range(members // SUB):
-            turn = (2 * LANES - STRIP - 2 * STRIP * group) % LANES
-            parts.append(jnp.where(edge, pltpu.roll(strip, turn, 1), 0.0))
-        return main + jnp.concatenate(parts, axis=0)
+            part = main[SUB * group:SUB * (group + 1)] + jnp.where(zone == group, strip, 0.0)
+            parts.append(pltpu.roll(part, LANES - 2 * STRIP * group, 1) if group else part)
+        return jnp.concatenate(parts, axis=0)
 
     copies = [pltpu.make_async_copy(out_ref.at[field], out_hbm.at[field], sems.at[field]) for field in range(3)]
     for field in range(3):
@@ -397,18 +427,14 @@
         in_specs=[pl.BlockSpec(memory_space=pl.ANY)] * 3,
         out_specs=(pl.BlockSpec(memory_space=pl.ANY),) * 3 + (vmem,) * 5,
         scratch_shapes=[
-            pltpu.VMEM((3 * SUB, 2, members, LANES), jnp.float32),
             pltpu.SMEM((both + PICKS,), jnp.int32),
-            pltpu.VMEM((3, 3 * SUB, SUB * JOINED, 2 * LANES), jnp.float32),
+            pltpu.VMEM((3, 3 * SUB, members + SUB, LANES), jnp.float32),
             pltpu.SMEM((NBATCH, count), jnp.int32),
             pltpu.VMEM((NBATCH, 1, count), jnp.int32),
             pltpu.VMEM((3, members * rows_dev, cols_dev), jnp.float32),
-            pltpu.VMEM((3, 3, rows_dev, members, cols_dev), jnp.float32),
-            pltpu.VMEM((3, rows_dev, SUB, cols_dev), jnp.float32),
-            pltpu.VMEM((3, rows_dev, SUB, cols_dev), jnp.float32),
             pltpu.SemaphoreType.DMA((3,)),
-            pltpu.SemaphoreType.DMA((groups // JOINED,)),
-            pltpu.SemaphoreType.DMA((groups // JOINED, 3)),
+            pltpu.SemaphoreType.DMA((3,)),
+            pltpu.SemaphoreType.DMA((3, 2)),
         ],
         compiler_params=pltpu.CompilerParams(vmem_limit_bytes=FORECAST_LIMIT),
         name="forecast",
@@ -429,21 +455,23 @@
     even_pairs = [(i, i ^ 1) for i in range(n_lon)]
     odd_pairs = [p for i in range(1, n_lon, 2) for p in ((i, (i + 1) % n_lon), ((i + 1) % n_lon, i))]
 
-    core_corner = lax.ppermute(core_strip, "lat", core_pairs)
+    cross_corner = lax.ppermute(cross_strip, "lat", cross_pairs)
     lat_bits = n_lat.bit_length() - 1
     lon_bits = n_lon.bit_length() - 1
-    for bit in reversed(range(lat_bits)):
+    for bit in reversed(range(1, lat_bits)):
         share = share + swap(share, "lat", n_lat, bit)
-        if bit == lat_bits - 1:
-            share, cross_strip = after(share, cross_strip)
-            cross_corner = lax.ppermute(cross_strip, "lat", cross_pairs)
+    corner_rows = core_strip.size // both
+    message = jnp.concatenate([share, core_strip.reshape(corner_rows, both)])
+    message = lax.ppermute(message, "lat", core_pairs)
+    share = share + message[:share.shape[0]]
+    core_corner = message[share.shape[0]:].reshape(core_strip.shape)
     share, cross_part, obs_value, obs_variance = after(share, cross_part, obs_value, obs_variance)
     from_cross = lax.ppermute(cross_part, "lat", cross_pairs)
     seen = jnp.stack([obs_value, obs_variance])
     strips = mid_strip + core_corner + cross_corner
     for bit in range(lon_bits):
         if bit == lon_bits - 2:
-            share, core_part = after(share, core_part)
+            share, core_part, seen = after(share, core_part, seen)
             from_core = lax.ppermute(core_part, "lat", core_pairs)
         if bit == lon_bits - 1:
             share, strips = after(share, strips)
@@ -484,6 +512,10 @@
         in_specs=[vmem] * 7,
         out_specs=vmem,
         scratch_shapes=[pltpu.VMEM((count, LANES), jnp.float32)] * 2
+        + [
+            pltpu.VMEM((NBATCH, 2, count, LANES), jnp.float32),
+            pltpu.VMEM((NBATCH * count // SUB, 2 * PANEL + 2, SUB, LANES), jnp.float32),
+        ]
         + [pltpu.SMEM((NBATCH, count), jnp.float32)] * 2
         + [pltpu.SemaphoreType.DMA((2,))],
         compiler_params=params,

time: 42.4 us -> 37.2 us (0.88)
  Pallas kernels: 20.1 us -> 15.4 us
  waiting for transfers between devices: 3.41 us -> 4.17 us
  local copies, waits for them, and re-layouts: 1.6 us -> 0.94 us
    pallas_call x1, Pallas kernels: 10.8 us -> 7.93 us  [body(): pl.pallas_call(functools.partial(filter_kernel, count, members), out_shap...]
    pallas_call x1, Pallas kernels: 8.01 us -> 6.19 us  [body(): pl.pallas_call(functools.partial(forecast_kernel, groups, members, n_lat,...]
    ppermute x1, starting transfers between devices: 2.31 us -> 0.93 us  [body(): from_core = lax.ppermute(core_part, 'lat', core_pairs)]
    ppermute x1, waiting for transfers between devices: 0.01 us -> 0.98 us  [body(): message = lax.ppermute(message, 'lat', core_pairs)]
    ppermute x5 -> x4, starting transfers between devices: 9.78 us -> 10.5 us  [swap(): return lax.ppermute(x, axis, [(i, i ^ 1 << bit) for i in range(size)])]
    unnamed x10 -> x12, local copies, waits for them, and re-layouts: 1.38 us -> 0.71 us
    ppermute x1, starting transfers between devices: 0.01 us -> 0.49 us  [body(): message = lax.ppermute(message, 'lat', core_pairs)]
    ppermute x5 -> x4, waiting for transfers between devices: 3.4 us -> 3.18 us  [swap(): return lax.ppermute(x, axis, [(i, i ^ 1 << bit) for i in range(size)])]
  transfers between devices with their start and end apart: 11 -> 10, of which waited for: 3 -> 4; matrix products, arithmetic and copies ran while one was open for 1% -> 1% of each run, Pallas kernels for 26% -> 21%
where the time goes in v2:
time: 37.2 us; the launch traced here: 37 us
  starting transfers between devices  16 us (43%)
  Pallas kernels  15.4 us (41%)
  waiting for transfers between devices  4.17 us (11%)
  local copies, waits for them, and re-layouts  0.94 us (3%)
    ppermute x4, starting transfers between devices, swap(): return lax.ppermute(x, axis, [(i, i ^ 1 << bit) for i in range(size)])  10.5 us
    pallas_call x1, Pallas kernels, body(): pl.pallas_call(functools.partial(filter_kernel, count, members), out_shap...  7.93 us
    pallas_call x1, Pallas kernels, body(): pl.pallas_call(functools.partial(forecast_kernel, groups, members, n_lat,...  6.19 us
    ppermute x4, waiting for transfers between devices, swap(): return lax.ppermute(x, axis, [(i, i ^ 1 << bit) for i in range(size)])  3.18 us
    ppermute x1, starting transfers between devices, body(): from_odd = lax.ppermute(strips, 'lon', odd_pairs)  1.53 us
    ppermute x1, starting transfers between devices, body(): from_even = lax.ppermute(strips, 'lon', even_pairs)  1.28 us
    pallas_call x1, Pallas kernels, body(): pl.pallas_call(functools.partial(apply_kernel, members), out_shape=array(...  1.26 us
    ppermute x1, waiting for transfers between devices, body(): message = lax.ppermute(message, 'lat', core_pairs)  0.98 us
  transfers between devices with their start and end apart: 10, of which 4 were waited for; matrix products, arithmetic and copies ran while one was open for 1% of the time, Pallas kernels for 21%

profile of v2, /device:TPU:0, one launch (start us, length us, event | category | flops | bytes accessed | tf_op | source)
XLA Modules:
  0.0 37.0 jit_solution(10369342751115743430)
XLA Ops:
  0.0 0.7 %copy-done.2 = s32[2,64,1]{1,2,0:T(1,128)S(1)} copy-done((s32[2,64,1]{1,2,0:T(1,128)S(1)}, s32[2,64,1]{1,2,0:T(1,128)}, u32[]{:S(2)}) %copy-start.2) | copy-done | bytes 536
  0.7 0.0 copy-done.1
  0.7 6.2 %forecast.1 = (f32[3,8,64,128]{3,2,1,0:T(8,128)}, f32[3,8,64,128]{3,2,1,0:T(8,128)}, f32[3,8,64,128]{3,2,1,0:T(8,128)}, f32[3,8,8,128]{3,2,1,0:T(8,128)S(1)}, f3...) custom-call(s32[2,64]{1,0:T(2,128)S(1)} %copy-done.1, ...), custom_call_target="tpu_custom_call" | custom-call | tf_op jit(solution)/shard_map/forecast/pallas_call | solution.py:422
  6.9 3.0 %collective-permute-start = (f32[72,128]{1,0:T(8,128)S(1)}, f32[72,128]{1,0:T(8,128)S(1)}, u32[]{:S(2)}, u32[]{:S(2)}) collective-permute-start(f32[72,128]{1,0:T(8,128)S(1)} %get-tuple-element.22), channel_id=1, source_target_pairs={{0,2},{1,3},{2,0},{3,1},{4,6},{5,7},{6,4},{7,5},{8,10},{9,11},{10,... | collective-permute-start | bytes 110600 | tf_op jit(solution)/shard_map/ppermute | solution.py:448
  9.9 0.7 %collective-permute-start.4 = (f32[3,8,8,128]{3,2,1,0:T(8,128)S(1)}, f32[3,8,8,128]{3,2,1,0:T(8,128)S(1)}, u32[]{:S(2)}, u32[]{:S(2)}) collective-permute-start(f32[3,8,8,128]{3,2,1,0:T(8,128)S(1)} %get-tuple-element.32), channel_id=1, source_target_pairs={{1,2},{2,1},{5,6},{6,5},{9,10},{10,9},{13,14},{14,13},{17,18},{18,... | collective-permute-start | bytes 294920 | tf_op jit(solution)/shard_map/ppermute | solution.py:458
  10.6 0.1 reshape.265
  10.7 0.1 fusion.11
  10.9 1.0 %collective-permute-done = f32[72,128]{1,0:T(8,128)S(1)} collective-permute-done((f32[72,128]{1,0:T(8,128)S(1)}, f32[72,128]{1,0:T(8,128)S(1)}, u32[]{:S(2)}, u32[]{:S(2)}) %collective-permute-start) | collective-permute-done | bytes 36896 | tf_op jit(solution)/shard_map/ppermute | solution.py:448
  11.9 0.5 %collective-permute-start.1 = (f32[264,128]{1,0:T(8,128)S(1)}, f32[264,128]{1,0:T(8,128)S(1)}, u32[]{:S(2)}, u32[]{:S(2)}) collective-permute-start(f32[264,128]{1,0:T(8,128)S(1)} %pad_maximum_fusion), channel_id=1, source_target_pairs={{0,1},{1,0},{2,3},{3,2},{4,5},{5,4},{6,7},{7,6},{8,9},{9,8},{10,11... | collective-permute-start | bytes 405512 | tf_op jit(solution)/shard_map/ppermute | solution.py:465
  12.4 1.0 %collective-permute-done.1 = f32[264,128]{1,0:T(8,128)S(1)} collective-permute-done((f32[264,128]{1,0:T(8,128)S(1)}, f32[264,128]{1,0:T(8,128)S(1)}, u32[]{:S(2)}, u32[]{:S(2)}) %collective-permute-start.1) | collective-permute-done | bytes 135200 | tf_op jit(solution)/shard_map/ppermute | solution.py:465
  13.4 2.1 %collective-permute-start.2 = (f32[72,128]{1,0:T(8,128)S(1)}, f32[72,128]{1,0:T(8,128)S(1)}, u32[]{:S(2)}, u32[]{:S(2)}) collective-permute-start(f32[72,128]{1,0:T(8,128)S(1)} %slice_add_fusion), channel_id=1, source_target_pairs={{0,4},{4,0},{8,12},{12,8},{16,20},{20,16},{24,28},{28,24},{1,5},{5... | collective-permute-start | bytes 110600 | tf_op jit(solution)/shard_map/ppermute | solution.py:448
  15.4 0.7 %collective-permute-start.7 = (f32[3,8,64,128]{3,2,1,0:T(8,128)}, f32[3,8,64,128]{3,2,1,0:T(8,128)S(1)}, u32[]{:S(2)}, u32[]{:S(2)}) collective-permute-start(f32[3,8,64,128]{3,2,1,0:T(8,128)} %get-tuple-element.37), channel_id=1, source_target_pairs={{1,2},{2,1},{5,6},{6,5},{9,10},{10,9},{13,14},{14,13},{17,18},{18,... | collective-permute-start | bytes 2359304 | tf_op jit(solution)/shard_map/ppermute | solution.py:469
  16.2 1.2 %collective-permute-done.2 = f32[72,128]{1,0:T(8,128)S(1)} collective-permute-done((f32[72,128]{1,0:T(8,128)S(1)}, f32[72,128]{1,0:T(8,128)S(1)}, u32[]{:S(2)}, u32[]{:S(2)}) %collective-permute-start.2) | collective-permute-done | bytes 36896 | tf_op jit(solution)/shard_map/ppermute | solution.py:448
  17.4 2.1 %collective-permute-start.3 = (f32[72,128]{1,0:T(8,128)S(1)}, f32[72,128]{1,0:T(8,128)S(1)}, u32[]{:S(2)}, u32[]{:S(2)}) collective-permute-start(f32[72,128]{1,0:T(8,128)S(1)} %add.161), channel_id=1, source_target_pairs={{0,8},{4,12},{8,0},{12,4},{16,24},{20,28},{24,16},{28,20},{1,9},{5... | collective-permute-start | bytes 110600 | tf_op jit(solution)/shard_map/ppermute | solution.py:448
  19.5 0.0 collective-permute-done.4
  19.5 0.9 %collective-permute-start.6 = (f32[3,8,64,128]{3,2,1,0:T(8,128)S(1)}, f32[3,8,64,128]{3,2,1,0:T(8,128)S(1)}, u32[]{:S(2)}, u32[]{:S(2)}) collective-permute-start(f32[3,8,64,128]{3,2,1,0:T(8,128)S(1)} %copy-done.5), channel_id=1, source_target_pairs={{0,1},{1,0},{2,3},{3,2},{4,5},{5,4},{6,7},{7,6},{8,9},{9,8},{10,11... | collective-permute-start | bytes 2359304 | tf_op jit(solution)/shard_map/ppermute | solution.py:475
  20.5 1.0 %collective-permute-done.3 = f32[72,128]{1,0:T(8,128)S(1)} collective-permute-done((f32[72,128]{1,0:T(8,128)S(1)}, f32[72,128]{1,0:T(8,128)S(1)}, u32[]{:S(2)}, u32[]{:S(2)}) %collective-permute-start.3) | collective-permute-done | bytes 36896 | tf_op jit(solution)/shard_map/ppermute | solution.py:448
  21.5 3.3 %collective-permute-start.5 = (f32[80,128]{1,0:T(8,128)S(1)}, f32[80,128]{1,0:T(8,128)S(1)}, u32[]{:S(2)}, u32[]{:S(2)}) collective-permute-start(f32[80,128]{1,0:T(8,128)S(1)} %pad_maximum_fusion.2), channel_id=1, source_target_pairs={{0,16},{4,20},{8,24},{12,28},{16,0},{20,4},{24,8},{28,12},{1,17},{... | collective-permute-start | bytes 122888 | tf_op jit(solution)/shard_map/ppermute | solution.py:448
  24.8 1.3 %collective-permute-start.8 = (f32[3,8,8,128]{3,2,1,0:T(8,128)S(1)}, f32[3,8,8,128]{3,2,1,0:T(8,128)S(1)}, u32[]{:S(2)}, u32[]{:S(2)}) collective-permute-start(f32[3,8,8,128]{3,2,1,0:T(8,128)S(1)} %add_add_fusion), channel_id=1, source_target_pairs={{0,4},{4,0},{8,12},{12,8},{16,20},{20,16},{24,28},{28,24},{1,5},{5... | collective-permute-start | bytes 294920 | tf_op jit(solution)/shard_map/ppermute | solution.py:478
  26.1 1.5 %collective-permute-start.9 = (f32[3,8,8,128]{3,2,1,0:T(8,128)S(1)}, f32[3,8,8,128]{3,2,1,0:T(8,128)S(1)}, u32[]{:S(2)}, u32[]{:S(2)}) collective-permute-start(f32[3,8,8,128]{3,2,1,0:T(8,128)S(1)} %add_add_fusion), channel_id=1, source_target_pairs={{4,8},{8,4},{12,16},{16,12},{20,24},{24,20},{28,0},{0,28},{5,9},{9... | collective-permute-start | bytes 294920 | tf_op jit(solution)/shard_map/ppermute | solution.py:479
  27.6 0.1 broadcast_in_dim.4.near_ref
  27.7 0.1 broadcast_in_dim.5.mine_ref
  27.8 7.9 %filter.1.change_ref = f32[64,64]{1,0:T(8,128)S(1)} custom-call(f32[2,2,64]{2,1,0:T(2,128)S(1)} %pad_maximum_fusion.3.seen_ref, f32[96,128]{1,0:T(8,128)S(1)} %pad_maximum_fusion.1.share_ref, f32[128,128]{1,0:T(8,128)S(1)} %get-tuple-element.49.geo_ref, f32[128,128]{1,0:T(8,128)S(1)} %get-tuple-element.48.geo_cols_ref, ...), custom_call_target="tpu_custom_call" | custom-call | tf_op jit(solution)/shard_map/filter/pallas_call | solution.py:509
  35.8 1.3 %apply.1 = f32[3,512,128]{2,1,0:T(8,128)} custom-call(f32[64,64]{1,0:T(8,128)S(1)} %filter.1.change_ref, f32[3,8,64,128]{3,2,1,0:T(8,128)S(1)} %copy-done, f32[3,8,64,128]{3,2,1,0:T(8,128)S(1)} %collective-permute-done.6.core_ref, f32[3,8,64,128]{3,2,1,0:T(8,128)S(1)} %collective-permute-done.7.cross_ref, ...), custom_call_target="tpu_custom_call" | custom-call | tf_op jit(solution)/shard_map/apply/pallas_call | solution.py:525
  (33 shorter events, 0.2 us)
Async XLA Ops:
  0.0 0.7 %copy-start.2 = (s32[2,64,1]{1,2,0:T(1,128)S(1)}, s32[2,64,1]{1,2,0:T(1,128)}, u32[]{:S(2)}) copy-start(s32[2,64,1]{1,2,0:T(1,128)} %param.9) | copy-start | bytes 1540
  0.0 0.7 %copy-start.1 = (s32[2,64]{1,0:T(2,128)S(1)}, s32[2,64]{1,0:T(2,128)}, u32[]{:S(2)}) copy-start(s32[2,64]{1,0:T(2,128)} %cell_hbm.1) | copy-start | bytes 1540
  6.9 5.0 %collective-permute-start = (f32[72,128]{1,0:T(8,128)S(1)}, f32[72,128]{1,0:T(8,128)S(1)}, u32[]{:S(2)}, u32[]{:S(2)}) collective-permute-start(f32[72,128]{1,0:T(8,128)S(1)} %get-tuple-element.22), channel_id=1, source_target_pairs={{0,2},{1,3},{2,0},{3,1},{4,6},{5,7},{6,4},{7,5},{8,10},{9,11},{10,... | collective-permute-start | bytes 110600 | tf_op jit(solution)/shard_map/ppermute | solution.py:448
  9.9 9.6 %collective-permute-start.4 = (f32[3,8,8,128]{3,2,1,0:T(8,128)S(1)}, f32[3,8,8,128]{3,2,1,0:T(8,128)S(1)}, u32[]{:S(2)}, u32[]{:S(2)}) collective-permute-start(f32[3,8,8,128]{3,2,1,0:T(8,128)S(1)} %get-tuple-element.32), channel_id=1, source_target_pairs={{1,2},{2,1},{5,6},{6,5},{9,10},{10,9},{13,14},{14,13},{17,18},{18,... | collective-permute-start | bytes 294920 | tf_op jit(solution)/shard_map/ppermute | solution.py:458
  11.9 1.5 %collective-permute-start.1 = (f32[264,128]{1,0:T(8,128)S(1)}, f32[264,128]{1,0:T(8,128)S(1)}, u32[]{:S(2)}, u32[]{:S(2)}) collective-permute-start(f32[264,128]{1,0:T(8,128)S(1)} %pad_maximum_fusion), channel_id=1, source_target_pairs={{0,1},{1,0},{2,3},{3,2},{4,5},{5,4},{6,7},{7,6},{8,9},{9,8},{10,11... | collective-permute-start | bytes 405512 | tf_op jit(solution)/shard_map/ppermute | solution.py:465
  13.4 2.8 %copy-start.3 = (f32[2,64]{1,0:T(2,128)S(1)}, f32[2,64]{1,0:T(2,128)}, u32[]{:S(2)}) copy-start(f32[2,64]{1,0:T(2,128)} %param.8) | copy-start | bytes 1540
  13.4 2.8 %copy-start.4 = (f32[2,64]{1,0:T(2,128)S(1)}, f32[2,64]{1,0:T(2,128)}, u32[]{:S(2)}) copy-start(f32[2,64]{1,0:T(2,128)} %param.7) | copy-start | bytes 1540
  13.4 6.2 %copy-start.5 = (f32[3,8,64,128]{3,2,1,0:T(8,128)S(1)}, f32[3,8,64,128]{3,2,1,0:T(8,128)}, u32[]{:S(2)}) copy-start(f32[3,8,64,128]{3,2,1,0:T(8,128)} %get-tuple-element.36) | copy-start | bytes 2359300
  13.4 22.4 %copy-start = (f32[3,8,64,128]{3,2,1,0:T(8,128)S(1)}, f32[3,8,64,128]{3,2,1,0:T(8,128)}, u32[]{:S(2)}) copy-start(f32[3,8,64,128]{3,2,1,0:T(8,128)} %get-tuple-element.35.mid_ref) | copy-start | bytes 2359300
  13.4 4.0 %collective-permute-start.2 = (f32[72,128]{1,0:T(8,128)S(1)}, f32[72,128]{1,0:T(8,128)S(1)}, u32[]{:S(2)}, u32[]{:S(2)}) collective-permute-start(f32[72,128]{1,0:T(8,128)S(1)} %slice_add_fusion), channel_id=1, source_target_pairs={{0,4},{4,0},{8,12},{12,8},{16,20},{20,16},{24,28},{28,24},{1,5},{5... | collective-permute-start | bytes 110600 | tf_op jit(solution)/shard_map/ppermute | solution.py:448
  15.4 20.3 %collective-permute-start.7 = (f32[3,8,64,128]{3,2,1,0:T(8,128)}, f32[3,8,64,128]{3,2,1,0:T(8,128)S(1)}, u32[]{:S(2)}, u32[]{:S(2)}) collective-permute-start(f32[3,8,64,128]{3,2,1,0:T(8,128)} %get-tuple-element.37), channel_id=1, source_target_pairs={{1,2},{2,1},{5,6},{6,5},{9,10},{10,9},{13,14},{14,13},{17,18},{18,... | collective-permute-start | bytes 2359304 | tf_op jit(solution)/shard_map/ppermute | solution.py:469
  17.4 4.0 %collective-permute-start.3 = (f32[72,128]{1,0:T(8,128)S(1)}, f32[72,128]{1,0:T(8,128)S(1)}, u32[]{:S(2)}, u32[]{:S(2)}) collective-permute-start(f32[72,128]{1,0:T(8,128)S(1)} %add.161), channel_id=1, source_target_pairs={{0,8},{4,12},{8,0},{12,4},{16,24},{20,28},{24,16},{28,20},{1,9},{5... | collective-permute-start | bytes 110600 | tf_op jit(solution)/shard_map/ppermute | solution.py:448
  19.5 16.2 %collective-permute-start.6 = (f32[3,8,64,128]{3,2,1,0:T(8,128)S(1)}, f32[3,8,64,128]{3,2,1,0:T(8,128)S(1)}, u32[]{:S(2)}, u32[]{:S(2)}) collective-permute-start(f32[3,8,64,128]{3,2,1,0:T(8,128)S(1)} %copy-done.5), channel_id=1, source_target_pairs={{0,1},{1,0},{2,3},{3,2},{4,5},{5,4},{6,7},{7,6},{8,9},{9,8},{10,11... | collective-permute-start | bytes 2359304 | tf_op jit(solution)/shard_map/ppermute | solution.py:475
  21.5 6.1 %collective-permute-start.5 = (f32[80,128]{1,0:T(8,128)S(1)}, f32[80,128]{1,0:T(8,128)S(1)}, u32[]{:S(2)}, u32[]{:S(2)}) collective-permute-start(f32[80,128]{1,0:T(8,128)S(1)} %pad_maximum_fusion.2), channel_id=1, source_target_pairs={{0,16},{4,20},{8,24},{12,28},{16,0},{20,4},{24,8},{28,12},{1,17},{... | collective-permute-start | bytes 122888 | tf_op jit(solution)/shard_map/ppermute | solution.py:448
  24.8 10.9 %collective-permute-start.8 = (f32[3,8,8,128]{3,2,1,0:T(8,128)S(1)}, f32[3,8,8,128]{3,2,1,0:T(8,128)S(1)}, u32[]{:S(2)}, u32[]{:S(2)}) collective-permute-start(f32[3,8,8,128]{3,2,1,0:T(8,128)S(1)} %add_add_fusion), channel_id=1, source_target_pairs={{0,4},{4,0},{8,12},{12,8},{16,20},{20,16},{24,28},{28,24},{1,5},{5... | collective-permute-start | bytes 294920 | tf_op jit(solution)/shard_map/ppermute | solution.py:478
  26.1 9.7 %collective-permute-start.9 = (f32[3,8,8,128]{3,2,1,0:T(8,128)S(1)}, f32[3,8,8,128]{3,2,1,0:T(8,128)S(1)}, u32[]{:S(2)}, u32[]{:S(2)}) collective-permute-start(f32[3,8,8,128]{3,2,1,0:T(8,128)S(1)} %add_add_fusion), channel_id=1, source_target_pairs={{4,8},{8,4},{12,16},{16,12},{20,24},{24,20},{28,0},{0,28},{5,9},{9... | collective-permute-start | bytes 294920 | tf_op jit(solution)/shard_map/ppermute | solution.py:479

commit v3 on v2

--- a/solution.py
+++ b/solution.py
@@ -455,39 +455,26 @@
     even_pairs = [(i, i ^ 1) for i in range(n_lon)]
     odd_pairs = [p for i in range(1, n_lon, 2) for p in ((i, (i + 1) % n_lon), ((i + 1) % n_lon, i))]
 
+    def exchange(x):
+        return lax.all_to_all(x, ("lon", "lat"), split_axis=0, concat_axis=0, tiled=True)
+
+    mask_row = jnp.sum(share[members:], axis=0).reshape(1, both)
+    pieces = exchange(share[:members].reshape(n_tiles, 1, members * both // n_tiles))
+    pieces, cross_strip, core_strip = after(pieces, cross_strip, core_strip)
     cross_corner = lax.ppermute(cross_strip, "lat", cross_pairs)
-    lat_bits = n_lat.bit_length() - 1
-    lon_bits = n_lon.bit_length() - 1
-    for bit in reversed(range(1, lat_bits)):
-        share = share + swap(share, "lat", n_lat, bit)
-    corner_rows = core_strip.size // both
-    message = jnp.concatenate([share, core_strip.reshape(corner_rows, both)])
-    message = lax.ppermute(message, "lat", core_pairs)
-    share = share + message[:share.shape[0]]
-    core_corner = message[share.shape[0]:].reshape(core_strip.shape)
-    share, cross_part, obs_value, obs_variance = after(share, cross_part, obs_value, obs_variance)
+    core_corner = lax.ppermute(core_strip, "lat", core_pairs)
+    piece = jnp.concatenate([jnp.sum(pieces, axis=0), mask_row], axis=1)
+    piece, obs_value, obs_variance = after(piece, obs_value, obs_variance)
+    seen = jnp.stack([obs_value, obs_variance])
+    all_pieces = exchange(jnp.broadcast_to(piece[None], (n_tiles,) + piece.shape))
+    strips = mid_strip + core_corner + cross_corner
+    all_pieces, strips, cross_part, core_part = after(all_pieces, strips, cross_part, core_part)
     from_cross = lax.ppermute(cross_part, "lat", cross_pairs)
-    seen = jnp.stack([obs_value, obs_variance])
-    strips = mid_strip + core_corner + cross_corner
-    for bit in range(lon_bits):
-        if bit == lon_bits - 2:
-            share, core_part, seen = after(share, core_part, seen)
-            from_core = lax.ppermute(core_part, "lat", core_pairs)
-        if bit == lon_bits - 1:
-            share, strips = after(share, strips)
-            from_even = lax.ppermute(strips, "lon", even_pairs)
-            from_odd = lax.ppermute(strips, "lon", odd_pairs)
-        other = swap(share, "lon", n_lon, bit)
-        if bit < lon_bits - 2:
-            share = share + other
-        else:
-            high = (lon >> bit) & 1
-            mine, theirs = share[members:], other[members:]
-            share = jnp.concatenate([
-                share[:members] + other[:members],
-                jnp.where(high == 1, theirs, mine),
-                jnp.where(high == 1, mine, theirs),
-            ])
+    from_core = lax.ppermute(core_part, "lat", core_pairs)
+    from_even = lax.ppermute(strips, "lon", even_pairs)
+    from_odd = lax.ppermute(strips, "lon", odd_pairs)
+    picked = all_pieces[:, 0, :members * both // n_tiles].reshape(members, both)
+    share = jnp.concatenate([picked, all_pieces[:, 0, members * both // n_tiles:]])
 
     cells = seen_cell.reshape(both)
     obs_row = cells // total_cols

time: 37.2 us -> 50.4 us (1.35)
  the two profiles are of different devices: /device:TPU:0 before, /device:TPU:1 now
where the time goes in v3:
time: 50.4 us; the launch traced here: 50.1 us
  starting transfers between devices  16.3 us (32%)
  Pallas kernels  15.4 us (31%)
  waiting for transfers between devices  15.1 us (30%)
  local copies, waits for them, and re-layouts  2.86 us (6%)
    all_to_all x2, waiting for transfers between devices, exchange(): lax.all_to_all(x, ('lon', 'lat'), split_axis=0, concat_axis=0, tiled=True)  14.2 us
    all_to_all x2, starting transfers between devices, exchange(): lax.all_to_all(x, ('lon', 'lat'), split_axis=0, concat_axis=0, tiled=True)  9.76 us
    pallas_call x1, Pallas kernels, body(): pl.pallas_call(functools.partial(filter_kernel, count, members), out_shap...  7.93 us
    pallas_call x1, Pallas kernels, body(): pl.pallas_call(functools.partial(forecast_kernel, groups, members, n_lat,...  6.22 us
    ppermute x1, starting transfers between devices, body(): cross_corner = lax.ppermute(cross_strip, 'lat', cross_pairs)  2.39 us
    ppermute x1, starting transfers between devices, body(): from_cross = lax.ppermute(cross_part, 'lat', cross_pairs)  2.08 us
    unnamed x12, local copies, waits for them, and re-layouts  1.38 us
    pallas_call x1, Pallas kernels, body(): pl.pallas_call(functools.partial(apply_kernel, members), out_shape=array(...  1.26 us
  transfers between devices with their start and end apart: 8, of which 3 were waited for; matrix products, arithmetic and copies ran while one was open for 2% of the time, Pallas kernels for 16%

profile of v3, /device:TPU:1, one launch (start us, length us, event | category | flops | bytes accessed | tf_op | source)
XLA Modules:
  0.0 50.1 jit_solution(3488853181994231899)
XLA Ops:
  0.0 0.7 %copy-done.2 = s32[2,64,1]{1,2,0:T(1,128)S(1)} copy-done((s32[2,64,1]{1,2,0:T(1,128)S(1)}, s32[2,64,1]{1,2,0:T(1,128)}, u32[]{:S(2)}) %copy-start.2) | copy-done | bytes 536
  0.7 6.2 %forecast.1 = (f32[3,8,64,128]{3,2,1,0:T(8,128)}, f32[3,8,64,128]{3,2,1,0:T(8,128)}, f32[3,8,64,128]{3,2,1,0:T(8,128)}, f32[3,8,8,128]{3,2,1,0:T(8,128)S(1)}, f3...) custom-call(s32[2,64]{1,0:T(2,128)S(1)} %copy-done.1, ...), custom_call_target="tpu_custom_call" | custom-call | tf_op jit(solution)/shard_map/forecast/pallas_call | solution.py:422
  6.9 0.6 %slice.12 = f32[64,128]{1,0:T(8,128)} slice(f32[72,128]{1,0:T(8,128)S(1)} %get-tuple-element.23), slice={[0:64], [0:128]} | slice | bytes 65536 | tf_op jit(solution)/shard_map/slice | solution.py:462
  7.5 7.1 %all-to-all-start = ((f32[32,1,256]{2,1,0:T(1,128)}), f32[32,1,256]{2,1,0:T(1,128)S(1)}, u32[]{:S(2)}, u32[]{:S(2)}) async-start(f32[32,1,256]{2,1,0:T(1,128)} %bitcast.3), calls=%async_computation | async-start | bytes 65536 | tf_op jit(solution)/shard_map/all_to_all | solution.py:459
  14.6 0.1 reshape.269
  14.8 6.9 %all-to-all-done = f32[32,1,256]{2,1,0:T(1,128)S(1)} async-done(((f32[32,1,256]{2,1,0:T(1,128)}), f32[32,1,256]{2,1,0:T(1,128)S(1)}, u32[]{:S(2)}, u32[]{:S(2)}) %all-to-all-start) | async-done | bytes 32800 | tf_op jit(solution)/shard_map/all_to_all | solution.py:459
  21.7 2.4 %collective-permute-start.1 = (f32[3,8,8,128]{3,2,1,0:T(8,128)S(1)}, f32[3,8,8,128]{3,2,1,0:T(8,128)S(1)}, u32[]{:S(2)}, u32[]{:S(2)}) collective-permute-start(f32[3,8,8,128]{3,2,1,0:T(8,128)S(1)} %get-tuple-element.32), channel_id=1, source_target_pairs={{1,2},{2,1},{5,6},{6,5},{9,10},{10,9},{13,14},{14,13},{17,18},{18,... | collective-permute-start | bytes 294920 | tf_op jit(solution)/shard_map/ppermute | solution.py:464
  24.1 0.1 collective-permute-start
  24.2 0.1 reduce_sum.20
  24.3 0.6 %broadcast_in_dim.9 = f32[32,1,384]{2,1,0:T(1,128)} broadcast(f32[384]{0:T(512)S(1)} %reduce.1), dimensions={2} | broadcast | bytes 50688 | tf_op jit(solution)/shard_map/broadcast_in_dim | solution.py:469
  25.0 2.7 %all-to-all-start.1 = ((f32[32,1,384]{2,1,0:T(1,128)}), f32[32,1,384]{2,1,0:T(1,128)S(1)}, u32[]{:S(2)}, u32[]{:S(2)}) async-start(f32[32,1,384]{2,1,0:T(1,128)} %broadcast_in_dim.9), calls=%async_computation.1 | async-start | bytes 98304 | tf_op jit(solution)/shard_map/all_to_all | solution.py:459
  27.7 7.3 %all-to-all-done.1 = f32[32,1,384]{2,1,0:T(1,128)S(1)} async-done(((f32[32,1,384]{2,1,0:T(1,128)}), f32[32,1,384]{2,1,0:T(1,128)S(1)}, u32[]{:S(2)}, u32[]{:S(2)}) %all-to-all-start.1) | async-done | bytes 49184 | tf_op jit(solution)/shard_map/all_to_all | solution.py:459
  35.0 0.4 collective-permute-start.2
  35.4 2.1 %collective-permute-start.3 = (f32[3,8,64,128]{3,2,1,0:T(8,128)}, f32[3,8,64,128]{3,2,1,0:T(8,128)S(1)}, u32[]{:S(2)}, u32[]{:S(2)}) collective-permute-start(f32[3,8,64,128]{3,2,1,0:T(8,128)} %get-tuple-element.39), channel_id=1, source_target_pairs={{1,2},{2,1},{5,6},{6,5},{9,10},{10,9},{13,14},{14,13},{17,18},{18,... | collective-permute-start | bytes 2359304 | tf_op jit(solution)/shard_map/ppermute | solution.py:472
  37.5 0.1 fusion.11
  37.6 0.5 %copy-done.5 = f32[2,64]{1,0:T(2,128)S(1)} copy-done((f32[2,64]{1,0:T(2,128)S(1)}, f32[2,64]{1,0:T(2,128)}, u32[]{:S(2)}) %copy-start.5) | copy-done | bytes 536
  38.2 0.2 copy-done.4
  38.3 0.5 collective-permute-start.4
  38.8 1.1 %collective-permute-start.5 = (f32[3,8,8,128]{3,2,1,0:T(8,128)S(1)}, f32[3,8,8,128]{3,2,1,0:T(8,128)S(1)}, u32[]{:S(2)}, u32[]{:S(2)}) collective-permute-start(f32[3,8,8,128]{3,2,1,0:T(8,128)S(1)} %add_add_fusion), channel_id=1, source_target_pairs={{4,8},{8,4},{12,16},{16,12},{20,24},{24,20},{28,0},{0,28},{5,9},{9... | collective-permute-start | bytes 294920 | tf_op jit(solution)/shard_map/ppermute | solution.py:475
  39.9 0.1 broadcast_in_dim.10.near_ref
  40.0 0.1 broadcast_in_dim.11.mine_ref
  40.1 7.9 %filter.1.change_ref = f32[64,64]{1,0:T(8,128)S(1)} custom-call(f32[2,2,64]{2,1,0:T(2,128)S(1)} %pad_maximum_fusion.1.seen_ref, f32[96,128]{1,0:T(8,128)S(1)} %pad_maximum_fusion.share_ref, f32[128,128]{1,0:T(8,128)S(1)} %get-tuple-element.47.geo_ref, f32[128,128]{1,0:T(8,128)S(1)} %get-tuple-element.46.geo_cols_ref, ...), custom_call_target="tpu_custom_call" | custom-call | tf_op jit(solution)/shard_map/filter/pallas_call | solution.py:496
  48.1 0.8 %collective-permute-done.3.cross_ref = f32[3,8,64,128]{3,2,1,0:T(8,128)S(1)} collective-permute-done((f32[3,8,64,128]{3,2,1,0:T(8,128)}, f32[3,8,64,128]{3,2,1,0:T(8,128)S(1)}, u32[]{:S(2)}, u32[]{:S(2)}) %collective-permute-start.3) | collective-permute-done | bytes 786464 | tf_op jit(solution)/shard_map/ppermute | solution.py:472
  48.9 1.3 %apply.1 = f32[3,512,128]{2,1,0:T(8,128)} custom-call(f32[64,64]{1,0:T(8,128)S(1)} %filter.1.change_ref, f32[3,8,64,128]{3,2,1,0:T(8,128)S(1)} %copy-done, f32[3,8,64,128]{3,2,1,0:T(8,128)S(1)} %collective-permute-done.2.core_ref, f32[3,8,64,128]{3,2,1,0:T(8,128)S(1)} %collective-permute-done.3.cross_ref, ...), custom_call_target="tpu_custom_call" | custom-call | tf_op jit(solution)/shard_map/apply/pallas_call | solution.py:512
  (29 shorter events, 0.2 us)
Async XLA Ops:
  0.0 0.7 %copy-start.2 = (s32[2,64,1]{1,2,0:T(1,128)S(1)}, s32[2,64,1]{1,2,0:T(1,128)}, u32[]{:S(2)}) copy-start(s32[2,64,1]{1,2,0:T(1,128)} %param.9) | copy-start | bytes 1540
  0.0 0.7 %copy-start.1 = (s32[2,64]{1,0:T(2,128)S(1)}, s32[2,64]{1,0:T(2,128)}, u32[]{:S(2)}) copy-start(s32[2,64]{1,0:T(2,128)} %cell_hbm.1) | copy-start | bytes 1540
  7.5 41.4 %copy-start = (f32[3,8,64,128]{3,2,1,0:T(8,128)S(1)}, f32[3,8,64,128]{3,2,1,0:T(8,128)}, u32[]{:S(2)}) copy-start(f32[3,8,64,128]{3,2,1,0:T(8,128)} %get-tuple-element.37.mid_ref) | copy-start | bytes 2359300
  7.5 14.2 %all-to-all-start = ((f32[32,1,256]{2,1,0:T(1,128)}), f32[32,1,256]{2,1,0:T(1,128)S(1)}, u32[]{:S(2)}, u32[]{:S(2)}) async-start(f32[32,1,256]{2,1,0:T(1,128)} %bitcast.3), calls=%async_computation | async-start | bytes 65536 | tf_op jit(solution)/shard_map/all_to_all | solution.py:459
  21.7 5.9 %collective-permute-start.1 = (f32[3,8,8,128]{3,2,1,0:T(8,128)S(1)}, f32[3,8,8,128]{3,2,1,0:T(8,128)S(1)}, u32[]{:S(2)}, u32[]{:S(2)}) collective-permute-start(f32[3,8,8,128]{3,2,1,0:T(8,128)S(1)} %get-tuple-element.32), channel_id=1, source_target_pairs={{1,2},{2,1},{5,6},{6,5},{9,10},{10,9},{13,14},{14,13},{17,18},{18,... | collective-permute-start | bytes 294920 | tf_op jit(solution)/shard_map/ppermute | solution.py:464
  24.1 3.5 %collective-permute-start = (f32[3,8,8,128]{3,2,1,0:T(8,128)S(1)}, f32[3,8,8,128]{3,2,1,0:T(8,128)S(1)}, u32[]{:S(2)}, u32[]{:S(2)}) collective-permute-start(f32[3,8,8,128]{3,2,1,0:T(8,128)S(1)} %get-tuple-element.31), channel_id=1, source_target_pairs={{0,1},{1,0},{2,3},{3,2},{4,5},{5,4},{6,7},{7,6},{8,9},{9,8},{10,11... | collective-permute-start | bytes 294920 | tf_op jit(solution)/shard_map/ppermute | solution.py:465
  25.0 10.0 %all-to-all-start.1 = ((f32[32,1,384]{2,1,0:T(1,128)}), f32[32,1,384]{2,1,0:T(1,128)S(1)}, u32[]{:S(2)}, u32[]{:S(2)}) async-start(f32[32,1,384]{2,1,0:T(1,128)} %broadcast_in_dim.9), calls=%async_computation.1 | async-start | bytes 98304 | tf_op jit(solution)/shard_map/all_to_all | solution.py:459
  35.0 3.4 %copy-start.3 = (f32[32,1,384]{2,1,0:T(1,128)}, f32[32,1,384]{2,1,0:T(1,128)S(1)}, u32[]{:S(2)}) copy-start(f32[32,1,384]{2,1,0:T(1,128)S(1)} %all-to-all-done.1) | copy-start | bytes 147460
  35.0 13.1 %collective-permute-start.2 = (f32[3,8,64,128]{3,2,1,0:T(8,128)}, f32[3,8,64,128]{3,2,1,0:T(8,128)S(1)}, u32[]{:S(2)}, u32[]{:S(2)}) collective-permute-start(f32[3,8,64,128]{3,2,1,0:T(8,128)} %get-tuple-element.38), channel_id=1, source_target_pairs={{0,1},{1,0},{2,3},{3,2},{4,5},{5,4},{6,7},{7,6},{8,9},{9,8},{10,11... | collective-permute-start | bytes 2359304 | tf_op jit(solution)/shard_map/ppermute | solution.py:473
  35.4 13.5 %collective-permute-start.3 = (f32[3,8,64,128]{3,2,1,0:T(8,128)}, f32[3,8,64,128]{3,2,1,0:T(8,128)S(1)}, u32[]{:S(2)}, u32[]{:S(2)}) collective-permute-start(f32[3,8,64,128]{3,2,1,0:T(8,128)} %get-tuple-element.39), channel_id=1, source_target_pairs={{1,2},{2,1},{5,6},{6,5},{9,10},{10,9},{13,14},{14,13},{17,18},{18,... | collective-permute-start | bytes 2359304 | tf_op jit(solution)/shard_map/ppermute | solution.py:472
  37.5 0.7 %copy-start.5 = (f32[2,64]{1,0:T(2,128)S(1)}, f32[2,64]{1,0:T(2,128)}, u32[]{:S(2)}) copy-start(f32[2,64]{1,0:T(2,128)} %param.7) | copy-start | bytes 1540
  37.6 0.7 %copy-start.4 = (f32[2,64]{1,0:T(2,128)S(1)}, f32[2,64]{1,0:T(2,128)}, u32[]{:S(2)}) copy-start(f32[2,64]{1,0:T(2,128)} %param.8) | copy-start | bytes 1540
  38.3 1.6 %slice-start = ((f32[32,1,384]{2,1,0:T(1,128)}), f32[32,1,256]{2,1,0:T(1,128)S(1)}, s32[]{:S(2)}) async-start(f32[32,1,384]{2,1,0:T(1,128)} %copy-done.3), calls=%async_computation.2 | async-start | bytes 65536 | tf_op jit(solution)/shard_map/slice | solution.py:476
  38.3 9.7 %collective-permute-start.4 = (f32[3,8,8,128]{3,2,1,0:T(8,128)S(1)}, f32[3,8,8,128]{3,2,1,0:T(8,128)S(1)}, u32[]{:S(2)}, u32[]{:S(2)}) collective-permute-start(f32[3,8,8,128]{3,2,1,0:T(8,128)S(1)} %add_add_fusion), channel_id=1, source_target_pairs={{0,4},{4,0},{8,12},{12,8},{16,20},{20,16},{24,28},{28,24},{1,5},{5... | collective-permute-start | bytes 294920 | tf_op jit(solution)/shard_map/ppermute | solution.py:474
  38.8 9.2 %collective-permute-start.5 = (f32[3,8,8,128]{3,2,1,0:T(8,128)S(1)}, f32[3,8,8,128]{3,2,1,0:T(8,128)S(1)}, u32[]{:S(2)}, u32[]{:S(2)}) collective-permute-start(f32[3,8,8,128]{3,2,1,0:T(8,128)S(1)} %add_add_fusion), channel_id=1, source_target_pairs={{4,8},{8,4},{12,16},{16,12},{20,24},{24,20},{28,0},{0,28},{5,9},{9... | collective-permute-start | bytes 294920 | tf_op jit(solution)/shard_map/ppermute | solution.py:475

commit v4 on v2

--- a/solution.py
+++ b/solution.py
@@ -24,10 +24,6 @@
 HIGHEST = lax.Precision.HIGHEST
 VMEM_LIMIT = 48 * 1024 * 1024
 FORECAST_LIMIT = 53 * 1024 * 1024 + 320 * 1024
-
-
-def dot(a, b):
-    return jnp.dot(a, b, precision=HIGHEST, preferred_element_type=jnp.float32)
 
 
 def dot_rows(a, b):
@@ -220,13 +216,18 @@
     def column(x, lane):
         return jnp.broadcast_to(x[:, lane:lane + 1], (SUB, LANES))
 
+    ready = None
     for first in range(0, count, PANEL):
         home, base = divmod(first, SUB)
         live = range(home, groups)
         inside = range(PANEL)
-        cols = [{i: column(own[i], first + q) for i in live} for q in inside]
+        close = live[:2]
+        cols = [{i: column(own[i], first + q) for i in close} for q in inside]
+        if ready is not None:
+            for q in inside:
+                cols[q][home] = ready[q]
         lams = [
-            {i: column(lam_cols[SUB * i:SUB * (i + 1)], offset + first + q) for i in live} for q in inside
+            {i: column(lam_cols[SUB * i:SUB * (i + 1)], offset + first + q) for i in close} for q in inside
         ]
         place = batch * groups + home
 
@@ -242,12 +243,27 @@
         keep(2 * PANEL + 1, other[home])
         for q in inside:
             keep(PANEL + q, lams[q][home])
+        ahead = home + 1 < groups
+        if ahead:
+            keep(2 * PANEL + 2, lams[PANEL - 1][home + 1])
         block = {(a, b): spread(b, base + a) for a in inside for b in inside if a <= b}
         rows_own = [spread(2 * PANEL, base + q) for q in inside]
         rows_other = [spread(2 * PANEL + 1, base + q) for q in inside]
         means = [column(mean, first + q) for q in inside]
         noises = [jnp.full((SUB, LANES), variances[batch, first + q], jnp.float32) for q in inside]
         total = block[0, 0] + (noises[0] + SMALL_EPSILON)
+        taken = []
+
+        def follow(i, t, now, links, kept):
+            shrink, alpha, beta, first_own, second_own, first_other, second_other = taken[t]
+            g = now[t]
+            u = links[t] * g
+            scaled = shrink * u
+            for q in range(t + 1, PANEL):
+                kept[q][i] = now[q] + (g * alpha[q] + scaled * beta[q])
+            own[i] = own[i] + (g * first_own + u * second_own)
+            other[i] = other[i] + (g * first_other + u * second_other)
+
         for t in inside:
             k = first + t
             noise = noises[t] * lax.rsqrt(noises[t])
@@ -283,14 +299,23 @@
             for a in range(t + 1, PANEL):
                 for b in range(a, PANEL):
                     block[a, b] = (block[a, b] + alpha[b] * block[t, a]) + alpha[a] * beta[b]
-            for i in live[1:]:
-                g = cols[t][i]
-                u = lams[t][i] * g
-                scaled = shrink * u
-                for q in range(t + 1, PANEL):
-                    cols[q][i] = cols[q][i] + (g * alpha[q] + scaled * beta[q])
-                own[i] = own[i] + (g * first_own + u * second_own)
-                other[i] = other[i] + (g * first_other + u * second_other)
+            if ahead and t == PANEL - 1:
+                g = cols[t][home + 1]
+                scaled = shrink * (lams[t][home + 1] * g)
+                for q in inside:
+                    v = shrink * (spread(2 * PANEL + 2, q) * edge[q])
+                    ready[q] = ready[q] + (g * v + scaled * (edge[q] + square * v))
+            taken.append((shrink, alpha, beta, first_own, second_own, first_other, second_other))
+            for i in close[1:]:
+                follow(i, t, [col[i] for col in cols], [lam[i] for lam in lams], cols)
+            if ahead and t == PANEL - 2:
+                ready = [column(own[home + 1], first + PANEL + q) for q in inside]
+                edge = [column(rows_own[t + 1], first + PANEL + q) for q in inside]
+        for i in live[2:]:
+            far_cols = [{i: column(own[i], first + q)} for q in inside]
+            far_lams = [column(lam_cols[SUB * i:SUB * (i + 1)], offset + first + q) for q in inside]
+            for t in inside:
+                follow(i, t, [col[i] for col in far_cols], far_lams, far_cols)
 
 
 def filter_kernel(
@@ -328,8 +353,8 @@
 
     mean, apart = begin(picked)
     first, second = apart[:, :count], apart[:, count:]
-    own = dot_rows(first, jnp.concatenate([first, eye], axis=1))
-    other = dot_rows(first, jnp.concatenate([second * math.sqrt(members - 1.0), eye], axis=1))
+    rows = dot_rows(first, jnp.concatenate([first, eye, second * math.sqrt(members - 1.0), eye], axis=1))
+    own, other = rows[:, :LANES], rows[:, LANES:]
     mean = jnp.broadcast_to(jnp.concatenate([mean[:, :count], mean[:, :count]], axis=1), (SUB, LANES))
     for copy in copies:
         copy.wait()
@@ -343,16 +368,15 @@
     change_one = moved[:, count:]
 
     mean, apart = begin(after)
-    own = dot_rows(apart, jnp.concatenate([apart, eye], axis=1))
-    other = jnp.concatenate([zeros, own[:, count:]], axis=1)
+    rows = dot_rows(apart, jnp.concatenate([apart, eye, zeros, eye + change_one], axis=1))
+    own, other = rows[:, :LANES], rows[:, LANES:]
     mean = jnp.broadcast_to(jnp.concatenate([mean, mean], axis=1), (SUB, LANES))
     batch_steps(
         values, variances, 1, count, own, other,
         jnp.where(left, swapped[count:], 0.0), jnp.where(left, 0.0, mine[count:]),
         lam_cols[count:], count, mean, spin, hist_other, hist_rows, lam_rows, spare,
     )
-    change_two = dot_rows(hist_rows[:, LANES - members:], hist_other[:, LANES - members:])
-    change_ref[...] = change_one + change_two + dot(change_two, change_one)
+    change_ref[...] = change_one + dot_rows(hist_rows[:, LANES - members:], hist_other[:, LANES - members:])
 
 
 def apply_kernel(members, change_ref, mid_ref, core_ref, cross_ref, even_ref, odd_ref, out_hbm, out_ref, sems):
@@ -514,7 +538,7 @@
         scratch_shapes=[pltpu.VMEM((count, LANES), jnp.float32)] * 2
         + [
             pltpu.VMEM((NBATCH, 2, count, LANES), jnp.float32),
-            pltpu.VMEM((NBATCH * count // SUB, 2 * PANEL + 2, SUB, LANES), jnp.float32),
+            pltpu.VMEM((NBATCH * count // SUB, 2 * PANEL + 3, SUB, LANES), jnp.float32),
         ]
         + [pltpu.SMEM((NBATCH, count), jnp.float32)] * 2
         + [pltpu.SemaphoreType.DMA((2,))],

time: 37.2 us -> 36.7 us (0.987)
  Pallas kernels: 15.4 us -> 14.9 us
    pallas_call x1, Pallas kernels: 7.93 us -> 7.44 us  [body(): pl.pallas_call(functools.partial(filter_kernel, count, members), out_shap...]
  transfers between devices with their start and end apart: 10 -> 10, of which waited for: 4 -> 4; matrix products, arithmetic and copies ran while one was open for 1% -> 1% of each run, Pallas kernels for 21% -> 20%
where the time goes in v4:
time: 36.7 us; the launch traced here: 36.5 us
  starting transfers between devices  16 us (44%)
  Pallas kernels  14.9 us (41%)
  waiting for transfers between devices  4.17 us (11%)
  local copies, waits for them, and re-layouts  0.94 us (3%)
    ppermute x4, starting transfers between devices, swap(): return lax.ppermute(x, axis, [(i, i ^ 1 << bit) for i in range(size)])  10.5 us
    pallas_call x1, Pallas kernels, body(): pl.pallas_call(functools.partial(filter_kernel, count, members), out_shap...  7.44 us
    pallas_call x1, Pallas kernels, body(): pl.pallas_call(functools.partial(forecast_kernel, groups, members, n_lat,...  6.19 us
    ppermute x4, waiting for transfers between devices, swap(): return lax.ppermute(x, axis, [(i, i ^ 1 << bit) for i in range(size)])  3.18 us
    ppermute x1, starting transfers between devices, body(): from_odd = lax.ppermute(strips, 'lon', odd_pairs)  1.53 us
    ppermute x1, starting transfers between devices, body(): from_even = lax.ppermute(strips, 'lon', even_pairs)  1.28 us
    pallas_call x1, Pallas kernels, body(): pl.pallas_call(functools.partial(apply_kernel, members), out_shape=array(...  1.26 us
    ppermute x1, waiting for transfers between devices, body(): message = lax.ppermute(message, 'lat', core_pairs)  0.98 us
  transfers between devices with their start and end apart: 10, of which 4 were waited for; matrix products, arithmetic and copies ran while one was open for 1% of the time, Pallas kernels for 20%

profile of v4, /device:TPU:0, one launch (start us, length us, event | category | flops | bytes accessed | tf_op | source)
XLA Modules:
  0.0 36.5 jit_solution(1522875064399572507)
XLA Ops:
  0.0 0.7 %copy-done.2 = s32[2,64,1]{1,2,0:T(1,128)S(1)} copy-done((s32[2,64,1]{1,2,0:T(1,128)S(1)}, s32[2,64,1]{1,2,0:T(1,128)}, u32[]{:S(2)}) %copy-start.2) | copy-done | bytes 536
  0.7 0.0 copy-done.1
  0.7 6.2 %forecast.1 = (f32[3,8,64,128]{3,2,1,0:T(8,128)}, f32[3,8,64,128]{3,2,1,0:T(8,128)}, f32[3,8,64,128]{3,2,1,0:T(8,128)}, f32[3,8,8,128]{3,2,1,0:T(8,128)S(1)}, f3...) custom-call(s32[2,64]{1,0:T(2,128)S(1)} %copy-done.1, ...), custom_call_target="tpu_custom_call" | custom-call | tf_op jit(solution)/shard_map/forecast/pallas_call | solution.py:446
  6.9 3.0 %collective-permute-start = (f32[72,128]{1,0:T(8,128)S(1)}, f32[72,128]{1,0:T(8,128)S(1)}, u32[]{:S(2)}, u32[]{:S(2)}) collective-permute-start(f32[72,128]{1,0:T(8,128)S(1)} %get-tuple-element.22), channel_id=1, source_target_pairs={{0,2},{1,3},{2,0},{3,1},{4,6},{5,7},{6,4},{7,5},{8,10},{9,11},{10,... | collective-permute-start | bytes 110600 | tf_op jit(solution)/shard_map/ppermute | solution.py:472
  9.9 0.7 %collective-permute-start.4 = (f32[3,8,8,128]{3,2,1,0:T(8,128)S(1)}, f32[3,8,8,128]{3,2,1,0:T(8,128)S(1)}, u32[]{:S(2)}, u32[]{:S(2)}) collective-permute-start(f32[3,8,8,128]{3,2,1,0:T(8,128)S(1)} %get-tuple-element.32), channel_id=1, source_target_pairs={{1,2},{2,1},{5,6},{6,5},{9,10},{10,9},{13,14},{14,13},{17,18},{18,... | collective-permute-start | bytes 294920 | tf_op jit(solution)/shard_map/ppermute | solution.py:482
  10.6 0.1 reshape.265
  10.7 0.1 fusion.11
  10.9 1.0 %collective-permute-done = f32[72,128]{1,0:T(8,128)S(1)} collective-permute-done((f32[72,128]{1,0:T(8,128)S(1)}, f32[72,128]{1,0:T(8,128)S(1)}, u32[]{:S(2)}, u32[]{:S(2)}) %collective-permute-start) | collective-permute-done | bytes 36896 | tf_op jit(solution)/shard_map/ppermute | solution.py:472
  11.9 0.5 %collective-permute-start.1 = (f32[264,128]{1,0:T(8,128)S(1)}, f32[264,128]{1,0:T(8,128)S(1)}, u32[]{:S(2)}, u32[]{:S(2)}) collective-permute-start(f32[264,128]{1,0:T(8,128)S(1)} %pad_maximum_fusion), channel_id=1, source_target_pairs={{0,1},{1,0},{2,3},{3,2},{4,5},{5,4},{6,7},{7,6},{8,9},{9,8},{10,11... | collective-permute-start | bytes 405512 | tf_op jit(solution)/shard_map/ppermute | solution.py:489
  12.4 1.0 %collective-permute-done.1 = f32[264,128]{1,0:T(8,128)S(1)} collective-permute-done((f32[264,128]{1,0:T(8,128)S(1)}, f32[264,128]{1,0:T(8,128)S(1)}, u32[]{:S(2)}, u32[]{:S(2)}) %collective-permute-start.1) | collective-permute-done | bytes 135200 | tf_op jit(solution)/shard_map/ppermute | solution.py:489
  13.4 2.1 %collective-permute-start.2 = (f32[72,128]{1,0:T(8,128)S(1)}, f32[72,128]{1,0:T(8,128)S(1)}, u32[]{:S(2)}, u32[]{:S(2)}) collective-permute-start(f32[72,128]{1,0:T(8,128)S(1)} %slice_add_fusion), channel_id=1, source_target_pairs={{0,4},{4,0},{8,12},{12,8},{16,20},{20,16},{24,28},{28,24},{1,5},{5... | collective-permute-start | bytes 110600 | tf_op jit(solution)/shard_map/ppermute | solution.py:472
  15.4 0.7 %collective-permute-start.7 = (f32[3,8,64,128]{3,2,1,0:T(8,128)}, f32[3,8,64,128]{3,2,1,0:T(8,128)S(1)}, u32[]{:S(2)}, u32[]{:S(2)}) collective-permute-start(f32[3,8,64,128]{3,2,1,0:T(8,128)} %get-tuple-element.37), channel_id=1, source_target_pairs={{1,2},{2,1},{5,6},{6,5},{9,10},{10,9},{13,14},{14,13},{17,18},{18,... | collective-permute-start | bytes 2359304 | tf_op jit(solution)/shard_map/ppermute | solution.py:493
  16.2 1.2 %collective-permute-done.2 = f32[72,128]{1,0:T(8,128)S(1)} collective-permute-done((f32[72,128]{1,0:T(8,128)S(1)}, f32[72,128]{1,0:T(8,128)S(1)}, u32[]{:S(2)}, u32[]{:S(2)}) %collective-permute-start.2) | collective-permute-done | bytes 36896 | tf_op jit(solution)/shard_map/ppermute | solution.py:472
  17.4 2.1 %collective-permute-start.3 = (f32[72,128]{1,0:T(8,128)S(1)}, f32[72,128]{1,0:T(8,128)S(1)}, u32[]{:S(2)}, u32[]{:S(2)}) collective-permute-start(f32[72,128]{1,0:T(8,128)S(1)} %add.161), channel_id=1, source_target_pairs={{0,8},{4,12},{8,0},{12,4},{16,24},{20,28},{24,16},{28,20},{1,9},{5... | collective-permute-start | bytes 110600 | tf_op jit(solution)/shard_map/ppermute | solution.py:472
  19.5 0.9 %collective-permute-start.6 = (f32[3,8,64,128]{3,2,1,0:T(8,128)S(1)}, f32[3,8,64,128]{3,2,1,0:T(8,128)S(1)}, u32[]{:S(2)}, u32[]{:S(2)}) collective-permute-start(f32[3,8,64,128]{3,2,1,0:T(8,128)S(1)} %copy-done.5), channel_id=1, source_target_pairs={{0,1},{1,0},{2,3},{3,2},{4,5},{5,4},{6,7},{7,6},{8,9},{9,8},{10,11... | collective-permute-start | bytes 2359304 | tf_op jit(solution)/shard_map/ppermute | solution.py:499
  20.5 1.0 %collective-permute-done.3 = f32[72,128]{1,0:T(8,128)S(1)} collective-permute-done((f32[72,128]{1,0:T(8,128)S(1)}, f32[72,128]{1,0:T(8,128)S(1)}, u32[]{:S(2)}, u32[]{:S(2)}) %collective-permute-start.3) | collective-permute-done | bytes 36896 | tf_op jit(solution)/shard_map/ppermute | solution.py:472
  21.5 3.3 %collective-permute-start.5 = (f32[80,128]{1,0:T(8,128)S(1)}, f32[80,128]{1,0:T(8,128)S(1)}, u32[]{:S(2)}, u32[]{:S(2)}) collective-permute-start(f32[80,128]{1,0:T(8,128)S(1)} %pad_maximum_fusion.2), channel_id=1, source_target_pairs={{0,16},{4,20},{8,24},{12,28},{16,0},{20,4},{24,8},{28,12},{1,17},{... | collective-permute-start | bytes 122888 | tf_op jit(solution)/shard_map/ppermute | solution.py:472
  24.8 1.3 %collective-permute-start.8 = (f32[3,8,8,128]{3,2,1,0:T(8,128)S(1)}, f32[3,8,8,128]{3,2,1,0:T(8,128)S(1)}, u32[]{:S(2)}, u32[]{:S(2)}) collective-permute-start(f32[3,8,8,128]{3,2,1,0:T(8,128)S(1)} %add_add_fusion), channel_id=1, source_target_pairs={{0,4},{4,0},{8,12},{12,8},{16,20},{20,16},{24,28},{28,24},{1,5},{5... | collective-permute-start | bytes 294920 | tf_op jit(solution)/shard_map/ppermute | solution.py:502
  26.1 1.5 %collective-permute-start.9 = (f32[3,8,8,128]{3,2,1,0:T(8,128)S(1)}, f32[3,8,8,128]{3,2,1,0:T(8,128)S(1)}, u32[]{:S(2)}, u32[]{:S(2)}) collective-permute-start(f32[3,8,8,128]{3,2,1,0:T(8,128)S(1)} %add_add_fusion), channel_id=1, source_target_pairs={{4,8},{8,4},{12,16},{16,12},{20,24},{24,20},{28,0},{0,28},{5,9},{9... | collective-permute-start | bytes 294920 | tf_op jit(solution)/shard_map/ppermute | solution.py:503
  27.6 0.0 collective-permute-done.5
  27.6 0.1 broadcast_in_dim.4.near_ref
  27.7 0.1 broadcast_in_dim.5.mine_ref
  27.8 7.4 %filter.1.change_ref = f32[64,64]{1,0:T(8,128)S(1)} custom-call(f32[2,2,64]{2,1,0:T(2,128)S(1)} %pad_maximum_fusion.3.seen_ref, f32[96,128]{1,0:T(8,128)S(1)} %pad_maximum_fusion.1.share_ref, f32[128,128]{1,0:T(8,128)S(1)} %get-tuple-element.49.geo_ref, f32[128,128]{1,0:T(8,128)S(1)} %get-tuple-element.48.geo_cols_ref, ...), custom_call_target="tpu_custom_call" | custom-call | tf_op jit(solution)/shard_map/filter/pallas_call | solution.py:533
  35.3 1.3 %apply.1 = f32[3,512,128]{2,1,0:T(8,128)} custom-call(f32[64,64]{1,0:T(8,128)S(1)} %filter.1.change_ref, f32[3,8,64,128]{3,2,1,0:T(8,128)S(1)} %copy-done, f32[3,8,64,128]{3,2,1,0:T(8,128)S(1)} %collective-permute-done.6.core_ref, f32[3,8,64,128]{3,2,1,0:T(8,128)S(1)} %collective-permute-done.7.cross_ref, ...), custom_call_target="tpu_custom_call" | custom-call | tf_op jit(solution)/shard_map/apply/pallas_call | solution.py:549
  (33 shorter events, 0.2 us)
Async XLA Ops:
  0.0 0.7 %copy-start.2 = (s32[2,64,1]{1,2,0:T(1,128)S(1)}, s32[2,64,1]{1,2,0:T(1,128)}, u32[]{:S(2)}) copy-start(s32[2,64,1]{1,2,0:T(1,128)} %param.9) | copy-start | bytes 1540
  0.0 0.7 %copy-start.1 = (s32[2,64]{1,0:T(2,128)S(1)}, s32[2,64]{1,0:T(2,128)}, u32[]{:S(2)}) copy-start(s32[2,64]{1,0:T(2,128)} %cell_hbm.1) | copy-start | bytes 1540
  6.9 5.0 %collective-permute-start = (f32[72,128]{1,0:T(8,128)S(1)}, f32[72,128]{1,0:T(8,128)S(1)}, u32[]{:S(2)}, u32[]{:S(2)}) collective-permute-start(f32[72,128]{1,0:T(8,128)S(1)} %get-tuple-element.22), channel_id=1, source_target_pairs={{0,2},{1,3},{2,0},{3,1},{4,6},{5,7},{6,4},{7,5},{8,10},{9,11},{10,... | collective-permute-start | bytes 110600 | tf_op jit(solution)/shard_map/ppermute | solution.py:472
  9.9 9.6 %collective-permute-start.4 = (f32[3,8,8,128]{3,2,1,0:T(8,128)S(1)}, f32[3,8,8,128]{3,2,1,0:T(8,128)S(1)}, u32[]{:S(2)}, u32[]{:S(2)}) collective-permute-start(f32[3,8,8,128]{3,2,1,0:T(8,128)S(1)} %get-tuple-element.32), channel_id=1, source_target_pairs={{1,2},{2,1},{5,6},{6,5},{9,10},{10,9},{13,14},{14,13},{17,18},{18,... | collective-permute-start | bytes 294920 | tf_op jit(solution)/shard_map/ppermute | solution.py:482
  11.9 1.5 %collective-permute-start.1 = (f32[264,128]{1,0:T(8,128)S(1)}, f32[264,128]{1,0:T(8,128)S(1)}, u32[]{:S(2)}, u32[]{:S(2)}) collective-permute-start(f32[264,128]{1,0:T(8,128)S(1)} %pad_maximum_fusion), channel_id=1, source_target_pairs={{0,1},{1,0},{2,3},{3,2},{4,5},{5,4},{6,7},{7,6},{8,9},{9,8},{10,11... | collective-permute-start | bytes 405512 | tf_op jit(solution)/shard_map/ppermute | solution.py:489
  13.4 2.8 %copy-start.3 = (f32[2,64]{1,0:T(2,128)S(1)}, f32[2,64]{1,0:T(2,128)}, u32[]{:S(2)}) copy-start(f32[2,64]{1,0:T(2,128)} %param.8) | copy-start | bytes 1540
  13.4 2.8 %copy-start.4 = (f32[2,64]{1,0:T(2,128)S(1)}, f32[2,64]{1,0:T(2,128)}, u32[]{:S(2)}) copy-start(f32[2,64]{1,0:T(2,128)} %param.7) | copy-start | bytes 1540
  13.4 6.2 %copy-start.5 = (f32[3,8,64,128]{3,2,1,0:T(8,128)S(1)}, f32[3,8,64,128]{3,2,1,0:T(8,128)}, u32[]{:S(2)}) copy-start(f32[3,8,64,128]{3,2,1,0:T(8,128)} %get-tuple-element.36) | copy-start | bytes 2359300
  13.4 21.9 %copy-start = (f32[3,8,64,128]{3,2,1,0:T(8,128)S(1)}, f32[3,8,64,128]{3,2,1,0:T(8,128)}, u32[]{:S(2)}) copy-start(f32[3,8,64,128]{3,2,1,0:T(8,128)} %get-tuple-element.35.mid_ref) | copy-start | bytes 2359300
  13.4 4.0 %collective-permute-start.2 = (f32[72,128]{1,0:T(8,128)S(1)}, f32[72,128]{1,0:T(8,128)S(1)}, u32[]{:S(2)}, u32[]{:S(2)}) collective-permute-start(f32[72,128]{1,0:T(8,128)S(1)} %slice_add_fusion), channel_id=1, source_target_pairs={{0,4},{4,0},{8,12},{12,8},{16,20},{20,16},{24,28},{28,24},{1,5},{5... | collective-permute-start | bytes 110600 | tf_op jit(solution)/shard_map/ppermute | solution.py:472
  15.4 19.8 %collective-permute-start.7 = (f32[3,8,64,128]{3,2,1,0:T(8,128)}, f32[3,8,64,128]{3,2,1,0:T(8,128)S(1)}, u32[]{:S(2)}, u32[]{:S(2)}) collective-permute-start(f32[3,8,64,128]{3,2,1,0:T(8,128)} %get-tuple-element.37), channel_id=1, source_target_pairs={{1,2},{2,1},{5,6},{6,5},{9,10},{10,9},{13,14},{14,13},{17,18},{18,... | collective-permute-start | bytes 2359304 | tf_op jit(solution)/shard_map/ppermute | solution.py:493
  17.4 4.0 %collective-permute-start.3 = (f32[72,128]{1,0:T(8,128)S(1)}, f32[72,128]{1,0:T(8,128)S(1)}, u32[]{:S(2)}, u32[]{:S(2)}) collective-permute-start(f32[72,128]{1,0:T(8,128)S(1)} %add.161), channel_id=1, source_target_pairs={{0,8},{4,12},{8,0},{12,4},{16,24},{20,28},{24,16},{28,20},{1,9},{5... | collective-permute-start | bytes 110600 | tf_op jit(solution)/shard_map/ppermute | solution.py:472
  19.5 15.7 %collective-permute-start.6 = (f32[3,8,64,128]{3,2,1,0:T(8,128)S(1)}, f32[3,8,64,128]{3,2,1,0:T(8,128)S(1)}, u32[]{:S(2)}, u32[]{:S(2)}) collective-permute-start(f32[3,8,64,128]{3,2,1,0:T(8,128)S(1)} %copy-done.5), channel_id=1, source_target_pairs={{0,1},{1,0},{2,3},{3,2},{4,5},{5,4},{6,7},{7,6},{8,9},{9,8},{10,11... | collective-permute-start | bytes 2359304 | tf_op jit(solution)/shard_map/ppermute | solution.py:499
  21.5 6.1 %collective-permute-start.5 = (f32[80,128]{1,0:T(8,128)S(1)}, f32[80,128]{1,0:T(8,128)S(1)}, u32[]{:S(2)}, u32[]{:S(2)}) collective-permute-start(f32[80,128]{1,0:T(8,128)S(1)} %pad_maximum_fusion.2), channel_id=1, source_target_pairs={{0,16},{4,20},{8,24},{12,28},{16,0},{20,4},{24,8},{28,12},{1,17},{... | collective-permute-start | bytes 122888 | tf_op jit(solution)/shard_map/ppermute | solution.py:472
  24.8 10.4 %collective-permute-start.8 = (f32[3,8,8,128]{3,2,1,0:T(8,128)S(1)}, f32[3,8,8,128]{3,2,1,0:T(8,128)S(1)}, u32[]{:S(2)}, u32[]{:S(2)}) collective-permute-start(f32[3,8,8,128]{3,2,1,0:T(8,128)S(1)} %add_add_fusion), channel_id=1, source_target_pairs={{0,4},{4,0},{8,12},{12,8},{16,20},{20,16},{24,28},{28,24},{1,5},{5... | collective-permute-start | bytes 294920 | tf_op jit(solution)/shard_map/ppermute | solution.py:502
  26.1 9.2 %collective-permute-start.9 = (f32[3,8,8,128]{3,2,1,0:T(8,128)S(1)}, f32[3,8,8,128]{3,2,1,0:T(8,128)S(1)}, u32[]{:S(2)}, u32[]{:S(2)}) collective-permute-start(f32[3,8,8,128]{3,2,1,0:T(8,128)S(1)} %add_add_fusion), channel_id=1, source_target_pairs={{4,8},{8,4},{12,16},{16,12},{20,24},{24,20},{28,0},{0,28},{5,9},{9... | collective-permute-start | bytes 294920 | tf_op jit(solution)/shard_map/ppermute | solution.py:503
